TPU v7x, 512 devices: a whole 4x4x16 slice. The times are simulated.
512 devices in a mesh: tile: 64 (over z, y), bands: 8 (over x, core).
Axes of the slice: x: 4, y: 4, z: 16, core: 2. Of those that a mesh axis runs over, the one named last changes fastest.
Arguments:
- scene_rows: bfloat16 [8, 8192, 768], P('bands', 'tile'), may hold values from -6 to 6
- row_dest: int32 [8192, 2], P('tile'), may hold values from 0 to 63, all different within a row; in each aligned block of 128 rows (0 to 127, 128 to 255, ...) at most 8 rows name the same one
- row_pos: int32 [8192, 2], P('tile'), may hold values from 0 to 1020
- along_taps: bfloat16 [8192, 2, 4], P('tile'), may hold values from 0.049804688 to 0.44921875
- across_taps: bfloat16 [8, 256, 8], P('bands'), may hold values from 0.019897461 to 0.29882812
- elevation: float32 [65536, 256], P(('tile', 'bands')), may hold values from -6 to 6
- pyramid_list: int32 [256, 3], P('tile'), may hold values from 0 to 63, as said below
Outputs:
- finished: bfloat16 [8, 65536, 256], P('bands', 'tile')
- pyramid: bfloat16 [8, 128, 256, 256], P('bands', 'tile')
Inputs may be any that keep to these rules, and one draw needn't show every extreme that they name: `row_dest`: among the 128 rows of one scene owner the two owners of a row differ, and no tile owner is named more than 8 times; that many is reached. `pyramid_list`: column 0 is the owner of tile g's own strip or of the strip just before or after it; one owner hands at most 2 tiles to each neighbouring owner; some owner hands 2 tiles to its left neighbour and some owner (possibly another) hands 2 to its right; column 1 lies below 2, column 2 below 4.
All inputs are finite; a program needn't handle non-finite values.
Results may differ from a plain program's by a relative error of at most 0.0049.
The roundings to bfloat16 on the way count: a program that leaves them out, or rounds other values in their place, can miss the bound.
Values may be sent and summed in bfloat16 or wider, within the bound.
No kernel may reach another device: no remote copies, remote signals or barrier semaphores. Data moves between devices by JAX's collectives and lax.ppermute only.
A program may use at most 192 MiB of HBM per device.

v0:
```python
import jax
import jax.numpy as jnp
from jax import lax
from jax.sharding import PartitionSpec as P

TILE_WIDTH = 256
WSRC = 768
KA = 4
KX = 8
PYR_DEV = 2
PMOST = 2


def extended(value, sides, width):
    for axis, dim in sides:
        size, length = (lax.axis_size(axis), value.shape[dim])
        up = [(i, (i + 1) % size) for i in range(size - 1)]
        down = [(j, i) for i, j in up]
        last = lax.slice_in_dim(value, length - width, length, axis=dim)
        first = lax.slice_in_dim(value, 0, width, axis=dim)
        before = lax.ppermute(last, axis, up)
        after = lax.ppermute(first, axis, down)
        value = jnp.concatenate([before, value, after], axis=dim)
    return value


def from_behind(value, axis, by):
    size = lax.axis_size(axis)
    pairs = [(i, i + by) for i in range(size) if 0 <= i + by < size]
    return lax.ppermute(value, axis, pairs)


def across_build(taps):
    source = jnp.arange(WSRC, dtype=jnp.int32)[:, None]
    columns = 3 * jnp.arange(TILE_WIDTH, dtype=jnp.int32)[None, :] - 2
    matrix = jnp.zeros((WSRC, TILE_WIDTH), jnp.float32)
    for tap in range(KX):
        matrix = jnp.where(
            source == columns + tap, taps[:, tap].astype(jnp.float32)[None, :], matrix
        )
    return matrix.astype(jnp.bfloat16)


def shade_of(padded):
    grid = jnp.pad(padded, ((0, 0), (1, 1)))
    grad_y = (grid[2:, 1:-1] - grid[:-2, 1:-1]) * 0.5
    grad_x = (grid[1:-1, 2:] - grid[1:-1, :-2]) * 0.5
    return (0.8660254 - 0.4 * grad_x - 0.3 * grad_y) / jnp.sqrt(
        1.0 + grad_x * grad_x + grad_y * grad_y
    )


def pyramid_downscale(output_tiles):
    half = output_tiles.shape[1] // 2
    values = output_tiles.astype(jnp.float32).reshape(output_tiles.shape[0], half, 2, half, 2)
    return jnp.sum(values, axis=(2, 4)) * 0.25


def shards(scene_rows, row_dest, row_pos, along_taps, across_taps, elevation, pyramid_list):
    owners_count = lax.axis_size("tile")
    rows_dev = row_dest.shape[0]
    routes_count = rows_dev * 2
    capacity = 4 * rows_dev // owners_count
    slots_count = owners_count * capacity
    tiles_dev = pyramid_list.shape[0]
    rows = scene_rows[0]
    across_matrix = across_build(across_taps[0])
    dest = row_dest.reshape(-1)
    positions = row_pos.reshape(-1)
    taps = along_taps.reshape(routes_count, KA)
    onehot = dest[:, None] == jnp.arange(owners_count, dtype=jnp.int32)[None, :]
    route_ids = jnp.arange(routes_count, dtype=jnp.int32)
    earlier = (route_ids[:, None] > route_ids[None, :]).astype(jnp.bfloat16)
    before = jnp.dot(earlier, onehot.astype(jnp.bfloat16), preferred_element_type=jnp.float32)
    ranking = jnp.sum(jnp.where(onehot, before, 0.0), axis=1).astype(jnp.int32)
    slot_of = dest * capacity + ranking
    route_of = jnp.zeros((slots_count,), jnp.int32).at[slot_of].set(route_ids)
    filled = jnp.zeros((slots_count,), jnp.bool_).at[slot_of].set(True)
    send_pos = jnp.where(filled, positions[route_of], 0)
    send_taps = jnp.where(filled[:, None], taps[route_of], jnp.zeros((), jnp.bfloat16))
    row_of = route_of // 2
    products = jnp.dot(rows, across_matrix, preferred_element_type=jnp.float32).astype(jnp.bfloat16)
    outgoing = jnp.where(filled[:, None], products[row_of], jnp.zeros((), jnp.bfloat16))
    across_in, in_pos, in_taps = (
        lax.all_to_all(outgoing, "tile", split_axis=0, concat_axis=0, tiled=True),
        lax.all_to_all(send_pos, "tile", split_axis=0, concat_axis=0, tiled=True),
        lax.all_to_all(send_taps, "tile", split_axis=0, concat_axis=0, tiled=True),
    )

    def strip_block(block_index):
        out_rows = block_index * TILE_WIDTH + jnp.arange(TILE_WIDTH, dtype=jnp.int32)
        distance = out_rows[:, None] - in_pos[None, :]
        weights_block = jnp.zeros((TILE_WIDTH, slots_count), jnp.bfloat16)
        for tap in range(KA):
            weights_block = jnp.where(distance == tap, in_taps[None, :, tap], weights_block)
        return jnp.dot(weights_block, across_in, preferred_element_type=jnp.float32)

    resampled = lax.map(strip_block, jnp.arange(tiles_dev, dtype=jnp.int32)).reshape(
        tiles_dev * TILE_WIDTH, TILE_WIDTH
    )
    padded = extended(elevation, ((("tile", "bands"), 0),), 1)
    shade = lax.all_gather(shade_of(padded), "bands", axis=0, tiled=True)
    finished = (resampled * shade).astype(jnp.bfloat16)
    output_tiles = finished.reshape(tiles_dev, TILE_WIDTH, TILE_WIDTH)
    halved_tiles = pyramid_downscale(output_tiles)
    codes = pyramid_list[:, 1] * 4 + pyramid_list[:, 2]
    offsets = pyramid_list[:, 0] - lax.axis_index("tile")
    children = [halved_tiles]
    child_codes = [jnp.where(offsets == 0, codes, -1)]
    slot_ids = jnp.arange(PMOST, dtype=jnp.int32)[:, None]
    for step in (1, -1):
        chosen = (offsets == step).astype(jnp.int32)
        ranking_tiles = jnp.cumsum(chosen) - chosen
        picked = (chosen[None, :] == 1) & (ranking_tiles[None, :] == slot_ids)
        codes_out = jnp.sum(jnp.where(picked, codes[None, :] + 1, 0), axis=1) - 1
        outgoing_tiles = jnp.sum(
            jnp.where(picked[:, :, None, None], output_tiles[None], jnp.zeros((), jnp.bfloat16)),
            axis=1,
        )
        received_rows_full, arrived_codes = from_behind((outgoing_tiles, codes_out), "tile", step)
        received_rows = pyramid_downscale(received_rows_full)
        children.append(received_rows)
        child_codes.append(arrived_codes)
    all_children = jnp.concatenate(children, axis=0)
    all_codes = jnp.concatenate(child_codes, axis=0)
    placement = (all_codes[:, None] == jnp.arange(PYR_DEV * 4, dtype=jnp.int32)[None, :]).astype(
        jnp.float32
    )
    summed = jnp.einsum("cp,cxy->pxy", placement, all_children, precision=lax.Precision.HIGHEST)
    half = TILE_WIDTH // 2
    summed = (
        summed.reshape(PYR_DEV, 2, 2, half, half)
        .transpose(0, 1, 3, 2, 4)
        .reshape(PYR_DEV, TILE_WIDTH, TILE_WIDTH)
    )
    return (finished[None], summed.astype(jnp.bfloat16)[None])


def solution(mesh):
    in_specs = (
        P("bands", "tile", None),
        P("tile", None),
        P("tile", None),
        P("tile", None, None),
        P("bands", None, None),
        P(("tile", "bands"), None),
        P("tile", None),
    )
    out_specs = (P("bands", "tile", None), P("bands", "tile", None, None))
    return jax.shard_map(shards, mesh=mesh, in_specs=in_specs, out_specs=out_specs, check_vma=False)
```

profile of v0, /device:TPU:24, one launch (start us, length us, event | category | flops | bytes accessed | tf_op | source)
XLA Modules:
  0.0 331.3 jit_solution(12312209620053777798)
XLA Ops:
  7.2 0.7 broadcast_multiply_fusion.3
  7.9 0.8 copy.45
  8.7 0.1 copy.44
  8.8 0.1 mul.114
  8.9 0.8 copy.46
  9.7 0.1 reshape.358
  9.9 0.1 eq.228
  10.0 0.2 fusion.23
  10.3 1.4 scatter_custom_fusion.1
  11.7 1.5 scatter_custom_fusion
  13.2 3.5 %gather_fusion = s32[512]{0:T(512)S(1)} fusion(s32[256]{0:T(256)S(1)} %reshape.358, s32[1024]{0:T(1024)S(1)} %get-tuple-element.78), kind=kCustom, calls=%fused_computation | custom fusion | bytes 6144 | tf_op jit(solution)/shard_map/gather | solution.py:79
  16.7 0.7 all_to_all.20
  17.4 18.5 %all-to-all-start = ((s32[64,8,1]{1,2,0:T(1,128)}), s32[64,8,1]{1,2,0:T(1,128)S(1)}, u32[]{:S(2)}, u32[]{:S(2)}) async-start(s32[64,8,1]{1,2,0:T(1,128)} %bitcast.4), calls=%async_computation | async-start | bytes 65536 | tf_op jit(solution)/shard_map/all_to_all | solution.py:86
  36.1 0.8 compare_reduce_fusion.1
  37.0 1.0 slice_convert_fusion.7
  38.0 0.7 fusion.22
  38.7 0.1 copy.51
  38.8 0.8 copy.48
  39.7 1.3 gather_fusion.1
  41.0 0.4 copy.49
  41.5 0.7 broadcast_select_fusion
  42.2 1.9 gather_fusion.2
  44.1 0.8 bitcast_select_fusion
  45.0 0.1 subtract_reduce_fusion
  45.1 3.4 %all-to-all-done = s32[64,8,1]{1,2,0:T(1,128)S(1)} async-done(((s32[64,8,1]{1,2,0:T(1,128)}), s32[64,8,1]{1,2,0:T(1,128)S(1)}, u32[]{:S(2)}, u32[]{:S(2)}) %all-to-all-start) | async-done | bytes 2080 | tf_op jit(solution)/shard_map/all_to_all | solution.py:86
  48.5 11.7 %all-to-all-start.1 = ((bf16[64,8,4]{1,2,0:T(4,128)(2,1)}), bf16[64,8,4]{1,2,0:T(4,128)(2,1)S(1)}, u32[]{:S(2)}, u32[]{:S(2)}) async-start(bf16[64,8,4]{1,2,0:T(4,128)(2,1)} %broadcast_select_fusion), calls=%async_computation.1 | async-start | bytes 131072 | tf_op jit(solution)/shard_map/all_to_all | solution.py:87
  60.2 1.0 select_reduce_fusion.2
  61.2 12.0 %all-to-all-done.1 = bf16[64,8,4]{1,2,0:T(4,128)(2,1)S(1)} async-done(((bf16[64,8,4]{1,2,0:T(4,128)(2,1)}), bf16[64,8,4]{1,2,0:T(4,128)(2,1)S(1)}, u32[]{:S(2)}, u32[]{:S(2)}) %all-to-all-start.1) | async-done | bytes 4128 | tf_op jit(solution)/shard_map/all_to_all | solution.py:87
  73.2 6.8 %all-to-all-start.2 = ((bf16[64,8,256]{2,1,0:T(8,128)(2,1)}), bf16[64,8,256]{2,1,0:T(8,128)(2,1)S(1)}, u32[]{:S(2)}, u32[]{:S(2)}) async-start(bf16[64,8,256]{2,1,0:T(8,128)(2,1)} %bitcast_select_fusion), calls=%async_computation.2 | async-start | bytes 524288 | tf_op jit(solution)/shard_map/all_to_all | solution.py:85
  80.0 0.1 select_reduce_fusion.4
  80.2 2.8 collective-permute-start.3
  83.0 0.7 fusion.64
  83.7 1.9 collective-permute-start.1
  85.6 2.4 collective-permute-start
  88.0 5.2 %collective-permute-start.2 = (s32[2]{0:T(128)S(1)}, s32[2]{0:T(128)S(1)}, u32[]{:S(2)}, u32[]{:S(2)}) collective-permute-start(s32[2]{0:T(128)S(1)} %broadcast_add_fusion.1), channel_id=1, source_target_pairs={{0,8},{8,16},{16,24},{24,32},{32,40},{40,48},{48,56},{56,64},{64,7... | collective-permute-start | bytes 32 | tf_op jit(solution)/shard_map/ppermute | solution.py:30
  93.3 1.0 select_maximum_fusion
  94.3 1.8 rsqrt_multiply_fusion
  96.1 0.5 broadcast.385
  96.6 0.6 reduce.25
  97.4 0.1 all_to_all.24
  97.5 2.3 all-to-all-done.2
  99.8 6.6 %while.10 = (s32[]{:T(128)}, f32[4,256,256]{2,1,0:T(8,128)S(1)}, s32[4]{0:T(128)S(1)}, s32[512]{0:T(512)S(1)}, bf16[512,4]{0,1:T(4,128)(2,1)S(1)}, /*index=5*/bf16[512,256]{1,0:T(8,128)(2,1)S(1)}, s32[]{:T(128)}, s32[1]{0:T(128)}) while((s32[]{:T(128)}, f32[4,256,256]{2,1,0:T(8,128)S(1)}, s32[4]{0:T(128)S(1)}, s32[512]{0:T(512)S(1)}, ...), condition=%wide.region_4.5_spmd, body=%wide.region_3.4_spmd.sunk | while | flops 68288768 | bytes 540797 | solution.py:98
  99.8 0.6 dynamic_slice.5
  101.1 0.4 fusion.71
  101.4 0.6 dynamic_slice.5
  102.7 0.4 fusion.71
  103.1 0.6 dynamic_slice.5
  104.4 0.4 fusion.71
  104.8 0.6 dynamic_slice.5
  106.0 0.4 fusion.71
  106.4 21.6 %all-gather.2.cloned.1.call-done = f32[1024,256]{1,0:T(8,128)} async-done(((f32[128,256]{1,0:T(8,128)}), f32[1024,256]{1,0:T(8,128)}) %all-gather.2.cloned.1.call-update) | async-done | bytes 1048592 | tf_op jit(solution)/shard_map/all_gather | solution.py:102
  128.0 1.4 fusion.24
  129.4 0.4 select_reduce_fusion.1
  129.9 2.7 collective-permute-start.5
  132.7 67.8 %reshape.373 = f32[4,128,2,128,2]{4,3,2,1,0:T(8,128)} reshape(bf16[1024,256]{1,0:T(8,128)(2,1)S(1)} %fusion.24) | data formatting | bytes 1572864 | tf_op jit(solution)/shard_map/convert_element_type | solution.py:55
  200.5 5.4 %collective-permute-start.4 = (bf16[2,256,256]{2,1,0:T(8,128)(2,1)S(1)}, bf16[2,256,256]{2,1,0:T(8,128)(2,1)S(1)}, u32[]{:S(2)}, u32[]{:S(2)}) collective-permute-start(bf16[2,256,256]{2,1,0:T(8,128)(2,1)S(1)} %get-tuple-element.39), channel_id=1, source_target_pairs={{0,8},{8,16},{16,24},{24,32},{32,40},{40,48},{48,56},{56,64},{64,7... | collective-permute-start | bytes 786440 | tf_op jit(solution)/shard_map/ppermute | solution.py:30
  205.9 21.0 %reduce_sum.81 = f32[4,128,128]{2,1,0:T(8,128)S(1)} reduce(f32[4,128,2,128,2]{4,3,2,1,0:T(8,128)} %reshape.373, f32[]{:T(128)} %constant.37.clone.1), dimensions={2,4}, to_apply=%region_9.10 | reduce | flops 196608 | bytes 1310724 | tf_op jit(solution)/shard_map/reduce_sum | solution.py:56
  227.0 34.6 %reshape.377 = f32[2,128,2,128,2]{4,3,2,1,0:T(8,128)} reshape(bf16[2,256,256]{2,1,0:T(8,128)(2,1)S(1)} %collective-permute-done.5) | data formatting | bytes 786432 | tf_op jit(solution)/shard_map/reshape | solution.py:55
  261.5 13.2 %reduce_sum.85 = f32[2,128,128]{2,1,0:T(8,128)S(1)} reduce(f32[2,128,2,128,2]{4,3,2,1,0:T(8,128)} %reshape.377, f32[]{:T(128)} %constant.37.clone.1), dimensions={2,4}, to_apply=%region_13.14 | reduce | flops 98304 | bytes 655364 | tf_op jit(solution)/shard_map/reduce_sum | solution.py:56
  274.8 34.6 %reshape.375 = f32[2,128,2,128,2]{4,3,2,1,0:T(8,128)} reshape(bf16[2,256,256]{2,1,0:T(8,128)(2,1)S(1)} %collective-permute-done.4) | data formatting | bytes 786432 | tf_op jit(solution)/shard_map/reshape | solution.py:55
  309.4 13.2 %reduce_sum.83 = f32[2,128,128]{2,1,0:T(8,128)S(1)} reduce(f32[2,128,2,128,2]{4,3,2,1,0:T(8,128)} %reshape.375, f32[]{:T(128)} %constant.37.clone.1), dimensions={2,4}, to_apply=%region_11.12 | reduce | flops 98304 | bytes 655364 | tf_op jit(solution)/shard_map/reduce_sum | solution.py:56
  322.7 0.7 convolution_convert_fusion
  323.4 0.2 copy.53
  323.6 0.9 convert_element_type.195
  (47 shorter events, 0.8 us)
Async XLA Ops:
  7.2 30.8 %copy-start = (bf16[1,128,768]{2,1,0:T(8,128)(2,1)S(1)}, bf16[1,128,768]{2,1,0:T(8,128)(2,1)}, u32[]{:S(2)}) copy-start(bf16[1,128,768]{2,1,0:T(8,128)(2,1)} %param.9) | copy-start | bytes 589828
  17.4 31.1 %all-to-all-start = ((s32[64,8,1]{1,2,0:T(1,128)}), s32[64,8,1]{1,2,0:T(1,128)S(1)}, u32[]{:S(2)}, u32[]{:S(2)}) async-start(s32[64,8,1]{1,2,0:T(1,128)} %bitcast.4), calls=%async_computation | async-start | bytes 65536 | tf_op jit(solution)/shard_map/all_to_all | solution.py:86
  48.5 24.7 %all-to-all-start.1 = ((bf16[64,8,4]{1,2,0:T(4,128)(2,1)}), bf16[64,8,4]{1,2,0:T(4,128)(2,1)S(1)}, u32[]{:S(2)}, u32[]{:S(2)}) async-start(bf16[64,8,4]{1,2,0:T(4,128)(2,1)} %broadcast_select_fusion), calls=%async_computation.1 | async-start | bytes 131072 | tf_op jit(solution)/shard_map/all_to_all | solution.py:87
  73.2 26.6 %all-to-all-start.2 = ((bf16[64,8,256]{2,1,0:T(8,128)(2,1)}), bf16[64,8,256]{2,1,0:T(8,128)(2,1)S(1)}, u32[]{:S(2)}, u32[]{:S(2)}) async-start(bf16[64,8,256]{2,1,0:T(8,128)(2,1)} %bitcast_select_fusion), calls=%async_computation.2 | async-start | bytes 524288 | tf_op jit(solution)/shard_map/all_to_all | solution.py:85
  80.0 48.0 %all-gather.2.cloned.1.call-start = ((), (), s32[]{:S(2)}) async-start(), calls=%async_computation.3 | async-start | bytes 1179648 | tf_op jit(solution)/shard_map/all_gather | solution.py:102
  80.2 52.4 %collective-permute-start.3 = (s32[2]{0:T(128)S(1)}, s32[2]{0:T(128)S(1)}, u32[]{:S(2)}, u32[]{:S(2)}) collective-permute-start(s32[2]{0:T(128)S(1)} %broadcast_add_fusion), channel_id=1, source_target_pairs={{8,0},{16,8},{24,16},{32,24},{40,32},{48,40},{56,48},{64,56},{72,6... | collective-permute-start | bytes 32 | tf_op jit(solution)/shard_map/ppermute | solution.py:30
  83.7 9.6 %collective-permute-start.1 = (f32[1,256]{1,0:T(1,128)S(1)}, f32[1,256]{1,0:T(1,128)S(1)}, u32[]{:S(2)}, u32[]{:S(2)}) collective-permute-start(f32[1,256]{1,0:T(1,128)S(1)} %get-tuple-element.63), channel_id=1, source_target_pairs={{1,0},{2,1},{3,2},{4,3},{5,4},{6,5},{7,6},{8,7},{9,8},{10,9},{11,1... | collective-permute-start | bytes 3080 | tf_op jit(solution)/shard_map/ppermute | solution.py:22
  85.6 7.6 %collective-permute-start = (f32[1,256]{1,0:T(1,128)S(1)}, f32[1,256]{1,0:T(1,128)S(1)}, u32[]{:S(2)}, u32[]{:S(2)}) collective-permute-start(f32[1,256]{1,0:T(1,128)S(1)} %get-tuple-element.64), channel_id=1, source_target_pairs={{0,1},{1,2},{2,3},{3,4},{4,5},{5,6},{6,7},{7,8},{8,9},{9,10},{10,1... | collective-permute-start | bytes 3080 | tf_op jit(solution)/shard_map/ppermute | solution.py:21
  88.0 44.6 %collective-permute-start.2 = (s32[2]{0:T(128)S(1)}, s32[2]{0:T(128)S(1)}, u32[]{:S(2)}, u32[]{:S(2)}) collective-permute-start(s32[2]{0:T(128)S(1)} %broadcast_add_fusion.1), channel_id=1, source_target_pairs={{0,8},{8,16},{16,24},{24,32},{32,40},{40,48},{48,56},{56,64},{64,7... | collective-permute-start | bytes 32 | tf_op jit(solution)/shard_map/ppermute | solution.py:30
  129.4 71.1 %copy-start.2 = (bf16[1024,256]{1,0:T(8,128)(2,1)}, bf16[1024,256]{1,0:T(8,128)(2,1)S(1)}, u32[]{:S(2)}) copy-start(bf16[1024,256]{1,0:T(8,128)(2,1)S(1)} %fusion.24) | copy-start | bytes 1572868
  129.9 97.1 %collective-permute-start.5 = (bf16[2,256,256]{2,1,0:T(8,128)(2,1)S(1)}, bf16[2,256,256]{2,1,0:T(8,128)(2,1)S(1)}, u32[]{:S(2)}, u32[]{:S(2)}) collective-permute-start(bf16[2,256,256]{2,1,0:T(8,128)(2,1)S(1)} %get-tuple-element.40), channel_id=1, source_target_pairs={{8,0},{16,8},{24,16},{32,24},{40,32},{48,40},{56,48},{64,56},{72,6... | collective-permute-start | bytes 786440 | tf_op jit(solution)/shard_map/ppermute | solution.py:30
  200.5 74.3 %collective-permute-start.4 = (bf16[2,256,256]{2,1,0:T(8,128)(2,1)S(1)}, bf16[2,256,256]{2,1,0:T(8,128)(2,1)S(1)}, u32[]{:S(2)}, u32[]{:S(2)}) collective-permute-start(bf16[2,256,256]{2,1,0:T(8,128)(2,1)S(1)} %get-tuple-element.39), channel_id=1, source_target_pairs={{0,8},{8,16},{16,24},{24,32},{32,40},{40,48},{48,56},{56,64},{64,7... | collective-permute-start | bytes 786440 | tf_op jit(solution)/shard_map/ppermute | solution.py:30
  274.8 49.7 %copy-start.1 = (bf16[1,128,768]{2,1,0:T(8,128)(2,1)S(1)}, bf16[1,128,768]{2,1,0:T(8,128)(2,1)}, u32[]{:S(2)}) copy-start(bf16[1,128,768]{2,1,0:T(8,128)(2,1)} %param.9) | copy-start | bytes 589828
Sparse Core Ops, SparseCore 0:
  96.2 31.7 all-gather.1
where the time goes:
time: 332 us; the launch traced here: 331 us
  local copies, waits for them, and re-layouts  156 us (47%)
  other arithmetic  58.5 us (18%)
  starting transfers between devices  57.4 us (17%)
  waiting for transfers between devices  39.3 us (12%)
  between operations  14.5 us (4%)
    reshape x2, local copies, waits for them, and re-layouts, pyramid_downscale(): output_tiles.astype(jnp.float32)  69.2 us
    convert_element_type x1, local copies, waits for them, and re-layouts, pyramid_downscale(): output_tiles.astype(jnp.float32)  67.8 us
    reduce_sum x3, other arithmetic, pyramid_downscale(): return jnp.sum(values, axis=(2, 4)) * 0.25  47.5 us
    all_gather x1, waiting for transfers between devices, shards(): shade = lax.all_gather(shade_of(padded), 'bands', axis=0, tiled=True)  21.6 us
    all_to_all x1, starting transfers between devices, shards(): lax.all_to_all(send_pos, 'tile', split_axis=0, concat_axis=0, tiled=True)  18.5 us
    ppermute x4, starting transfers between devices, from_behind(): return lax.ppermute(value, axis, pairs)  16.1 us
    all_to_all x1, waiting for transfers between devices, shards(): lax.all_to_all(send_taps, 'tile', split_axis=0, concat_axis=0, tiled=True)  12 us
    all_to_all x1, starting transfers between devices, shards(): lax.all_to_all(send_taps, 'tile', split_axis=0, concat_axis=0, tiled=True)  11.7 us
  transfers between devices with their start and end apart: 10, of which 4 were waited for; matrix products, arithmetic and copies ran while one was open for 48% of the time, Pallas kernels for 0%

commit v1 on v0

v1 whole, which is shorter than its diff:
```python
import jax
import jax.numpy as jnp
from jax import lax
from jax.experimental import pallas as pl
from jax.experimental.pallas import tpu as pltpu
from jax.sharding import PartitionSpec as P

TILE = 256
WSRC = 768
KA = 4
KX = 8
OWNERS = 64
CAP = 8
ROWS = 128
TILES = 4
HALF = 128
CHUNK = 2 * CAP + 2
GROUP = 8 * CHUNK
FIELDS = 2 + KA
PAYLOAD = 2 * HALF + 16
F32 = jnp.float32
BF16 = jnp.bfloat16
I32 = jnp.int32
VMEM = pl.BlockSpec(memory_space=pltpu.VMEM)
SMEM = pl.BlockSpec(memory_space=pltpu.SMEM)
PARAMS = pltpu.CompilerParams(vmem_limit_bytes=24 * 1024 * 1024)


def iota(shape, axis):
    return lax.broadcasted_iota(I32, shape, axis)


def dot(a, b):
    return jnp.dot(a, b, preferred_element_type=F32)


def dot_t(a, b):
    return lax.dot_general(a, b, (((1,), (1,)), ((), ())), preferred_element_type=F32)


def ones_where(mask):
    return jnp.where(mask, F32(1), F32(0))


def prep_kernel(rows_ref, dest_ref, pos_ref, along_ref, across_ref, out_ref):
    taps = across_ref[...].astype(F32)
    products = []
    for half in range(2):
        first, live = (0, 0) if half == 0 else (256, 368)
        shape = (400, HALF)
        offset = iota(shape, 0) + live - 3 * (iota(shape, 1) + half * HALF) + 2
        matrix = jnp.zeros(shape, F32)
        for tap in range(KX):
            matrix = jnp.where(offset == tap, taps[tap : tap + 1, half * HALF : (half + 1) * HALF], matrix)
        matrix = matrix.astype(BF16)
        empty = jnp.zeros((112, HALF), BF16)
        matrix = jnp.concatenate([matrix, empty] if half == 0 else [empty, matrix], axis=0)
        products.append(dot(rows_ref[:, first : first + 512], matrix).astype(BF16))
    products = jnp.concatenate(products, axis=0)

    owner = iota((OWNERS, ROWS), 0)
    d0, d1 = dest_ref[0:1, :], dest_ref[1:2, :]
    on0, on1 = ones_where(owner == d0), ones_where(owner == d1)
    b0, b1 = on0.astype(BF16), on1.astype(BF16)
    earlier = ones_where(iota((ROWS, ROWS), 0) < iota((ROWS, ROWS), 1)).astype(BF16)
    rank0 = jnp.sum(on0 * dot(b0, earlier), axis=0, keepdims=True).astype(I32)
    before1 = dot(b1, earlier) + dot(b0, jnp.ones((ROWS, ROWS), BF16))
    rank1 = jnp.sum(on1 * before1, axis=0, keepdims=True).astype(I32)

    slot = iota((CAP, ROWS), 0)
    meta = jnp.zeros((OWNERS, HALF), F32)
    for t, (on, rank) in enumerate(((b0, rank0), (b1, rank1))):
        position = pos_ref[t : t + 1, :]
        along = along_ref[t].astype(F32)
        fields = [(position >> 4).astype(F32), (position & 15).astype(F32)]
        fields += [along[k : k + 1, :] for k in range(KA)]
        spread = [jnp.where(slot == rank, field, F32(0)) for field in fields]
        spread.append(jnp.zeros((HALF - FIELDS * CAP, ROWS), F32))
        meta = meta + dot_t(on, jnp.concatenate(spread, axis=0).astype(BF16))
    meta = meta.astype(BF16)

    base0, base1 = d0 * CHUNK + 2 * rank0, d1 * CHUNK + 2 * rank1
    row = iota((GROUP, ROWS), 0)
    row_o, col_o = iota((GROUP, OWNERS), 0), iota((GROUP, OWNERS), 1)
    for g in range(OWNERS // 8):
        n0, n1 = base0 - g * GROUP, base1 - g * GROUP
        left = ones_where((row == n0) | (row == n1))
        right = ones_where((row == n0 + 1) | (row == n1 + 1))
        pick = jnp.concatenate([left, right], axis=1).astype(BF16)
        place = ones_where(row_o + g * GROUP == col_o * CHUNK + 2 * CAP).astype(BF16)
        out_ref[g * GROUP : (g + 1) * GROUP, :] = (dot(pick, products) + dot(place, meta)).astype(BF16)


def shade_kernel(z_ref, before_ref, after_ref, out_ref):
    z = z_ref[...]
    shape = z.shape
    row, col = iota(shape, 0), iota(shape, 1)
    up = jnp.where(row == 0, before_ref[...], pltpu.roll(z, 1, 0))
    down = jnp.where(row == shape[0] - 1, after_ref[...], pltpu.roll(z, shape[0] - 1, 0))
    left = jnp.where(col == 0, F32(0), pltpu.roll(z, 1, 1))
    right = jnp.where(col == shape[1] - 1, F32(0), pltpu.roll(z, shape[1] - 1, 1))
    grad_y = (down - up) * 0.5
    grad_x = (right - left) * 0.5
    shade = (0.8660254 - 0.4 * grad_x - 0.3 * grad_y) / jnp.sqrt(1.0 + grad_x * grad_x + grad_y * grad_y)
    out_ref[...] = shade.astype(BF16)


def main_kernel(recv_ref, mine_ref, theirs_ref, list_ref, out_ref, part_ref, up_ref, down_ref, across_ref, meta_ref):
    row, col = iota((GROUP, GROUP), 0), iota((GROUP, GROUP), 1)
    slot = row & 63
    target = jnp.where(
        row < 2 * 64,
        CHUNK * (slot >> 3) + 2 * (slot & 7) + (row >> 6),
        jnp.where(row < 2 * 64 + 8, CHUNK * slot + 2 * CAP, -1),
    )
    pick = ones_where(col == target).astype(BF16)
    for g in range(OWNERS // 8):
        parts = dot(pick, recv_ref[g * GROUP : (g + 1) * GROUP, :])
        across_ref[g * 64 : (g + 1) * 64, :HALF] = parts[:64].astype(BF16)
        across_ref[g * 64 : (g + 1) * 64, HALF:] = parts[64:128].astype(BF16)
        meta_ref[g * 8 : (g + 1) * 8, :] = parts[128:136]
    slots = OWNERS * CAP
    meta = meta_ref[...]
    rolled = [meta] + [pltpu.roll(meta, HALF - CAP * f, 1) for f in range(1, FIELDS)]
    spread = ones_where(iota((HALF, slots), 0) == (iota((HALF, slots), 1) & 7)).astype(BF16)
    wide = dot(jnp.concatenate(rolled, axis=0).astype(BF16), spread)
    own_lane = iota((OWNERS, slots), 0) == (iota((OWNERS, slots), 1) >> 3)
    fields = [
        jnp.sum(jnp.where(own_lane, wide[f * OWNERS : (f + 1) * OWNERS], F32(0)), axis=0, keepdims=True)
        for f in range(FIELDS)
    ]
    block, inner = fields[0].astype(I32), fields[1].astype(I32)
    diff = iota((16, slots), 0) - inner
    here, after = jnp.zeros((16, slots), F32), jnp.zeros((16, slots), F32)
    for tap in range(KA):
        here = jnp.where(diff == tap, fields[2 + tap], here)
        after = jnp.where(diff + 16 == tap, fields[2 + tap], after)
    block = jnp.broadcast_to(block, (16, slots))

    tile_me = lax.axis_index("tile")
    band_me = lax.axis_index("bands")
    core_me, x_me = lax.rem(band_me, 2), lax.div(band_me, 2)
    rows_of = ones_where(iota((HALF, TILE), 0) == (iota((HALF, TILE), 1) >> 1)).astype(BF16)
    cols_of = ones_where((iota((TILE, HALF), 0) >> 1) == iota((TILE, HALF), 1)).astype(BF16)
    part_ref[...] = jnp.zeros(part_ref.shape, F32)
    up_ref[...] = jnp.zeros(up_ref.shape, BF16)
    down_ref[...] = jnp.zeros(down_ref.shape, BF16)
    across = across_ref[...]
    counts = [jnp.int32(0), jnp.int32(0)]
    codes = [[jnp.int32(0), jnp.int32(0)], [jnp.int32(0), jnp.int32(0)]]
    for tile in range(TILES):
        weights = jnp.concatenate(
            [
                jnp.where(block == p, here, jnp.where(block == p - 1, after, F32(0))).astype(BF16)
                for p in range(16 * tile, 16 * tile + 16)
            ],
            axis=0,
        )
        resampled = dot(weights, across)
        mine = mine_ref[tile ^ x_me].astype(F32)
        theirs = theirs_ref[tile ^ x_me].astype(F32)
        top = jnp.where(core_me == 0, mine, theirs)
        bottom = jnp.where(core_me == 0, theirs, mine)
        finished = (resampled * jnp.concatenate([top, bottom], axis=0)).astype(BF16)
        out_ref[tile * TILE : (tile + 1) * TILE, :] = finished
        pairs = dot(rows_of, finished)
        high = pairs.astype(BF16)
        low = (pairs - high.astype(F32)).astype(BF16)
        reduced = (dot(high, cols_of) + dot(low, cols_of)) * 0.25
        offset = list_ref[tile, 0] - tile_me
        code = list_ref[tile, 1] * 4 + list_ref[tile, 2]

        @pl.when(offset == 0)
        def _(reduced=reduced, code=code):
            part_ref[code] = part_ref[code] + reduced

        for way, (step, ref) in enumerate(((1, up_ref), (-1, down_ref))):
            goes = offset == step
            rank = jnp.minimum(counts[way], 1)

            @pl.when(goes)
            def _(reduced=reduced, rank=rank, ref=ref):
                ref[pl.ds(pl.multiple_of(rank * HALF, HALF), HALF), :] = reduced.astype(BF16)

            for s in range(2):
                codes[way][s] = jnp.where(goes & (rank == s), code + 1, codes[way][s])
            counts[way] = counts[way] + goes.astype(I32)
    eighth = iota((16, HALF), 0) < 8
    for way, ref in enumerate((up_ref, down_ref)):
        ref[2 * HALF :, :] = jnp.where(eighth, codes[way][0], codes[way][1]).astype(F32).astype(BF16)


def combine_kernel(part_ref, up_ref, down_ref, out_ref):
    arrived = []
    for ref in (up_ref, down_ref):
        codes = ref[2 * HALF :, :].astype(F32)
        for s in range(2):
            arrived.append((codes[8 * s : 8 * s + 1], ref[s * HALF : (s + 1) * HALF, :].astype(F32)))
    for place in range(8):
        total = part_ref[place]
        for code, tile in arrived:
            total = total + jnp.where(code == F32(place + 1), tile, F32(0))
        level, quadrant = divmod(place, 4)
        top, left = quadrant // 2 * HALF, quadrant % 2 * HALF
        out_ref[level, top : top + HALF, left : left + HALF] = total.astype(BF16)


def call(kernel, outs, ins, scratch=(), cost=None):
    return pl.pallas_call(
        kernel,
        out_shape=outs,
        in_specs=ins,
        out_specs=jax.tree.map(lambda _: VMEM, outs),
        scratch_shapes=scratch,
        compiler_params=PARAMS,
        cost_estimate=cost,
    )


def shift(value, axes, by):
    size = lax.axis_size(axes)
    return lax.ppermute(value, axes, [(i, i + by) for i in range(size) if 0 <= i + by < size])


def exchange(value, mask):
    return lax.ppermute(value, "bands", [(i, i ^ mask) for i in range(lax.axis_size("bands"))])


def shards(scene_rows, row_dest, row_pos, along_taps, across_taps, elevation, pyramid_list):
    shape = jax.ShapeDtypeStruct
    outgoing = call(prep_kernel, shape((OWNERS * CHUNK, HALF), BF16), [VMEM] * 5)(
        scene_rows[0],
        row_dest.T,
        row_pos.T,
        along_taps.transpose(1, 2, 0),
        across_taps[0].T,
    )
    outgoing, elevation = lax.optimization_barrier((outgoing, elevation))
    units = outgoing.reshape(OWNERS * CHUNK // 2, 2, HALF)
    received = lax.all_to_all(units, "tile", split_axis=0, concat_axis=0, tiled=True)
    received = received.reshape(OWNERS * CHUNK, HALF)

    both = ("tile", "bands")
    before = shift(elevation[ROWS - 1 :], both, 1)
    after = shift(elevation[:1], both, -1)
    shade = call(shade_kernel, shape((ROWS, TILE), BF16), [VMEM] * 3)(elevation, before, after)
    mine = jnp.stack([shade, exchange(shade, 2), exchange(shade, 4), exchange(shade, 6)])
    theirs = exchange(mine, 1)

    finished, part, up, down = call(
        main_kernel,
        (
            shape((TILES * TILE, TILE), BF16),
            shape((8, HALF, HALF), F32),
            shape((PAYLOAD, HALF), BF16),
            shape((PAYLOAD, HALF), BF16),
        ),
        [VMEM, VMEM, VMEM, SMEM],
        [pltpu.VMEM((OWNERS * CAP, TILE), BF16), pltpu.VMEM((OWNERS, HALF), F32)],
    )(received, mine, theirs, pyramid_list)
    pyramid = call(combine_kernel, shape((2, TILE, TILE), BF16), [VMEM] * 3)(
        part, shift(up, "tile", 1), shift(down, "tile", -1)
    )
    return (finished[None], pyramid[None])


def solution(mesh):
    in_specs = (
        P("bands", "tile", None),
        P("tile", None),
        P("tile", None),
        P("tile", None, None),
        P("bands", None, None),
        P(("tile", "bands"), None),
        P("tile", None),
    )
    out_specs = (P("bands", "tile", None), P("bands", "tile", None, None))
    return jax.shard_map(shards, mesh=mesh, in_specs=in_specs, out_specs=out_specs, check_vma=False)
```

time: 332 us -> 74.2 us (0.22)
  the two profiles are of different devices: /device:TPU:24 before, /device:TPU:122 now
where the time goes in v1:
time: 74.2 us; the launch traced here: 73.7 us
  starting transfers between devices  48.6 us (65%)
  waiting for transfers between devices  15.4 us (21%)
  Pallas kernels  7.26 us (10%)
  local copies, waits for them, and re-layouts  1.63 us (2%)
  between operations  0.79 us (1%)
    all_to_all x1, starting transfers between devices, shards(): lax.all_to_all(units, 'tile', split_axis=0, concat_axis=0, tiled=True)  17.3 us
    ppermute x4, starting transfers between devices, shift(): lax.ppermute(value, axes, [(i, i + by) for i in range(size) if 0 <= i + b...  16.5 us
    ppermute x4, starting transfers between devices, exchange(): lax.ppermute(value, 'bands', [(i, i ^ mask) for i in range(lax.axis_size(...  14.8 us
    ppermute x4, waiting for transfers between devices, shift(): lax.ppermute(value, axes, [(i, i + by) for i in range(size) if 0 <= i + b...  10.1 us
    ppermute x4, waiting for transfers between devices, exchange(): lax.ppermute(value, 'bands', [(i, i ^ mask) for i in range(lax.axis_size(...  5.36 us
    pallas_call x1, Pallas kernels, shards(): call(main_kernel, (shape((TILES * TILE, TILE), BF16), shape((8, HALF, HAL...  4.38 us
    pallas_call x1, Pallas kernels, shards(): call(prep_kernel, shape((OWNERS * CHUNK, HALF), BF16), [VMEM] * 5)  1.79 us
    unnamed x14, local copies, waits for them, and re-layouts  1.63 us
  transfers between devices with their start and end apart: 9, of which 5 were waited for; matrix products, arithmetic and copies ran while one was open for 0% of the time, Pallas kernels for 0%

profile of v1, /device:TPU:122, one launch (start us, length us, event | category | flops | bytes accessed | tf_op | source)
XLA Modules:
  0.0 73.7 jit_solution(15081351052661189624)
XLA Ops:
  0.6 0.0 copy-start.6
  0.6 0.0 copy-start.2
  0.7 0.0 copy-start.3
  0.7 0.0 copy-start.5
  0.7 0.6 copy-done.6
  1.3 0.0 copy-done.2
  1.3 0.0 copy-done.3
  1.3 0.0 copy-done.5
  1.4 0.0 copy-start
  1.4 0.9 %copy-done = bf16[1,128,768]{2,1,0:T(8,128)(2,1)S(1)} copy-done((bf16[1,128,768]{2,1,0:T(8,128)(2,1)S(1)}, bf16[1,128,768]{2,1,0:T(8,128)(2,1)}, u32[]{:S(2)}) %copy-start) | copy-done | bytes 196632
  2.3 1.8 %shard_map.86 = bf16[1152,128]{1,0:T(8,128)(2,1)} custom-call(bf16[128,768]{1,0:T(8,128)(2,1)S(1)} %bitcast.17, s32[2,128]{1,0:T(2,128)S(1)} %bitcast.20, s32[2,128]{1,0:T(2,128)S(1)} %bitcast.21, bf16[2,4,128]{2,1,0:T(4,128)(2,1)S(1)} %bitcast.19, bf16[8,256]{1,0:T(8,128)(2,1)S(1)} %bitcast.18), custom_call_target="tpu_custom_call" | custom-call | tf_op jit(solution)/shard_map/pallas_call | solution.py:231
  4.1 0.0 copy-start.1
  4.1 17.3 %all-to-all-start = ((bf16[576,2,128]{2,1,0:T(2,128)(2,1)}), bf16[576,2,128]{2,1,0:T(2,128)(2,1)S(1)}, u32[]{:S(2)}, u32[]{:S(2)}) async-start(bf16[576,2,128]{2,1,0:T(2,128)(2,1)} %bitcast.6), calls=%async_computation | async-start | bytes 589824 | tf_op jit(solution)/shard_map/all_to_all | solution.py:240
  21.4 0.0 copy-done.1
  21.4 1.9 %collective-permute-start.1 = (f32[1,256]{1,0:T(1,128)S(1)}, f32[1,256]{1,0:T(1,128)S(1)}, u32[]{:S(2)}, u32[]{:S(2)}) collective-permute-start(f32[1,256]{1,0:T(1,128)S(1)} %get-tuple-element.14), channel_id=1, source_target_pairs={{1,0},{2,1},{3,2},{4,3},{5,4},{6,5},{7,6},{8,7},{9,8},{10,9},{11,1... | collective-permute-start | bytes 3080 | tf_op jit(solution)/shard_map/ppermute | solution.py:222
  23.3 2.4 %collective-permute-start = (f32[1,256]{1,0:T(1,128)S(1)}, f32[1,256]{1,0:T(1,128)S(1)}, u32[]{:S(2)}, u32[]{:S(2)}) collective-permute-start(f32[1,256]{1,0:T(1,128)S(1)} %get-tuple-element.15), channel_id=1, source_target_pairs={{0,1},{1,2},{2,3},{3,4},{4,5},{5,6},{6,7},{7,8},{8,9},{9,10},{10,1... | collective-permute-start | bytes 3080 | tf_op jit(solution)/shard_map/ppermute | solution.py:222
  25.7 0.0 collective-permute-done.1.after_ref
  25.7 2.5 %collective-permute-done.before_ref = f32[1,256]{1,0:T(1,128)S(1)} collective-permute-done((f32[1,256]{1,0:T(1,128)S(1)}, f32[1,256]{1,0:T(1,128)S(1)}, u32[]{:S(2)}, u32[]{:S(2)}) %collective-permute-start) | collective-permute-done | bytes 1056 | tf_op jit(solution)/shard_map/ppermute | solution.py:222
  28.2 0.2 shard_map.87
  28.4 3.4 %collective-permute-start.4 = (bf16[128,256]{1,0:T(8,128)(2,1)S(1)}, bf16[128,256]{1,0:T(8,128)(2,1)S(1)}, u32[]{:S(2)}, u32[]{:S(2)}) collective-permute-start(bf16[128,256]{1,0:T(8,128)(2,1)S(1)} %shard_map.87), channel_id=1, source_target_pairs={{0,6},{1,7},{2,4},{3,5},{4,2},{5,3},{6,0},{7,1},{8,14},{9,15},{10,... | collective-permute-start | bytes 196616 | tf_op jit(solution)/shard_map/ppermute | solution.py:226
  31.8 7.0 %collective-permute-start.3 = (bf16[128,256]{1,0:T(8,128)(2,1)S(1)}, bf16[128,256]{1,0:T(8,128)(2,1)S(1)}, u32[]{:S(2)}, u32[]{:S(2)}) collective-permute-start(bf16[128,256]{1,0:T(8,128)(2,1)S(1)} %shard_map.87), channel_id=1, source_target_pairs={{0,4},{1,5},{2,6},{3,7},{4,0},{5,1},{6,2},{7,3},{8,12},{9,13},{10,... | collective-permute-start | bytes 196616 | tf_op jit(solution)/shard_map/ppermute | solution.py:226
  38.9 1.9 %collective-permute-start.2 = (bf16[128,256]{1,0:T(8,128)(2,1)S(1)}, bf16[128,256]{1,0:T(8,128)(2,1)S(1)}, u32[]{:S(2)}, u32[]{:S(2)}) collective-permute-start(bf16[128,256]{1,0:T(8,128)(2,1)S(1)} %shard_map.87), channel_id=1, source_target_pairs={{0,2},{1,3},{2,0},{3,1},{4,6},{5,7},{6,4},{7,5},{8,10},{9,11},{10,... | collective-permute-start | bytes 196616 | tf_op jit(solution)/shard_map/ppermute | solution.py:226
  40.8 0.0 collective-permute-done.4
  40.8 0.3 collective-permute-done.3
  41.1 3.9 %collective-permute-done.2 = bf16[128,256]{1,0:T(8,128)(2,1)S(1)} collective-permute-done((bf16[128,256]{1,0:T(8,128)(2,1)S(1)}, bf16[128,256]{1,0:T(8,128)(2,1)S(1)}, u32[]{:S(2)}, u32[]{:S(2)}) %collective-permute-start.2) | collective-permute-done | bytes 65568 | tf_op jit(solution)/shard_map/ppermute | solution.py:226
  45.0 0.0 copy-start.4
  45.1 2.4 %collective-permute-start.5 = (bf16[4,128,256]{2,1,0:T(8,128)(2,1)S(1)}, bf16[4,128,256]{2,1,0:T(8,128)(2,1)S(1)}, u32[]{:S(2)}, u32[]{:S(2)}) collective-permute-start(bf16[4,128,256]{2,1,0:T(8,128)(2,1)S(1)} %pad_maximum_fusion.mine_ref), channel_id=1, source_target_pairs={{0,1},{1,0},{2,3},{3,2},{4,5},{5,4},{6,7},{7,6},{8,9},{9,8},{10,11... | collective-permute-start | bytes 786440 | tf_op jit(solution)/shard_map/ppermute | solution.py:226
  47.5 1.1 %collective-permute-done.5.theirs_ref = bf16[4,128,256]{2,1,0:T(8,128)(2,1)S(1)} collective-permute-done((bf16[4,128,256]{2,1,0:T(8,128)(2,1)S(1)}, bf16[4,128,256]{2,1,0:T(8,128)(2,1)S(1)}, u32[]{:S(2)}, u32[]{:S(2)}) %collective-permute-start.5) | collective-permute-done | bytes 262176 | tf_op jit(solution)/shard_map/ppermute | solution.py:226
  48.7 0.0 all-to-all-done
  48.7 0.0 copy-done.4
  48.7 4.4 %shard_map.88 = (bf16[1024,256]{1,0:T(8,128)(2,1)}, f32[8,128,128]{2,1,0:T(8,128)S(1)}, bf16[272,128]{1,0:T(8,128)(2,1)S(1)}, bf16[272,128]{1,0:T(8,128)(2,1)S(1)}) custom-call(bf16[1152,128]{1,0:T(8,128)(2,1)S(1)} %bitcast.15, bf16[4,128,256]{2,1,0:T(8,128)(2,1)S(1)} %pad_maximum_fusion.mine_ref, ...), custom_call_target="tpu_custom_call" | custom-call | tf_op jit(solution)/shard_map/pallas_call | solution.py:250
  53.1 10.3 %collective-permute-start.6 = (bf16[272,128]{1,0:T(8,128)(2,1)S(1)}, bf16[272,128]{1,0:T(8,128)(2,1)S(1)}, u32[]{:S(2)}, u32[]{:S(2)}) collective-permute-start(bf16[272,128]{1,0:T(8,128)(2,1)S(1)} %get-tuple-element.12), channel_id=1, source_target_pairs={{0,8},{8,16},{16,24},{24,32},{32,40},{40,48},{48,56},{56,64},{64,7... | collective-permute-start | bytes 208904 | tf_op jit(solution)/shard_map/ppermute | solution.py:222
  63.3 1.9 %collective-permute-start.7 = (bf16[272,128]{1,0:T(8,128)(2,1)S(1)}, bf16[272,128]{1,0:T(8,128)(2,1)S(1)}, u32[]{:S(2)}, u32[]{:S(2)}) collective-permute-start(bf16[272,128]{1,0:T(8,128)(2,1)S(1)} %get-tuple-element.13), channel_id=1, source_target_pairs={{8,0},{16,8},{24,16},{32,24},{40,32},{48,40},{56,48},{64,56},{72,6... | collective-permute-start | bytes 208904 | tf_op jit(solution)/shard_map/ppermute | solution.py:222
  65.3 0.0 collective-permute-done.6.up_ref
  65.3 7.6 %collective-permute-done.7.down_ref = bf16[272,128]{1,0:T(8,128)(2,1)S(1)} collective-permute-done((bf16[272,128]{1,0:T(8,128)(2,1)S(1)}, bf16[272,128]{1,0:T(8,128)(2,1)S(1)}, u32[]{:S(2)}, u32[]{:S(2)}) %collective-permute-start.7) | collective-permute-done | bytes 69664 | tf_op jit(solution)/shard_map/ppermute | solution.py:222
  72.9 0.9 %shard_map.89 = bf16[2,256,256]{2,1,0:T(8,128)(2,1)} custom-call(f32[8,128,128]{2,1,0:T(8,128)S(1)} %get-tuple-element.11.part_ref, bf16[272,128]{1,0:T(8,128)(2,1)S(1)} %collective-permute-done.6.up_ref, bf16[272,128]{1,0:T(8,128)(2,1)S(1)} %collective-permute-done.7.down_ref), custom_call_target="tpu_custom_call" | custom-call | tf_op jit(solution)/shard_map/pallas_call | solution.py:261
  (2 shorter events, 0.0 us)
Async XLA Ops:
  0.6 0.7 copy-start.6
  0.6 0.7 copy-start.2
  0.7 0.7 copy-start.3
  0.7 0.7 copy-start.5
  1.4 0.9 %copy-start = (bf16[1,128,768]{2,1,0:T(8,128)(2,1)S(1)}, bf16[1,128,768]{2,1,0:T(8,128)(2,1)}, u32[]{:S(2)}) copy-start(bf16[1,128,768]{2,1,0:T(8,128)(2,1)} %param.7) | copy-start | bytes 589828
  4.1 17.3 %copy-start.1 = (f32[128,256]{1,0:T(8,128)S(1)}, f32[128,256]{1,0:T(8,128)}, u32[]{:S(2)}) copy-start(f32[128,256]{1,0:T(8,128)} %z_ref) | copy-start | bytes 393220
  4.1 44.6 %all-to-all-start = ((bf16[576,2,128]{2,1,0:T(2,128)(2,1)}), bf16[576,2,128]{2,1,0:T(2,128)(2,1)S(1)}, u32[]{:S(2)}, u32[]{:S(2)}) async-start(bf16[576,2,128]{2,1,0:T(2,128)(2,1)} %bitcast.6), calls=%async_computation | async-start | bytes 589824 | tf_op jit(solution)/shard_map/all_to_all | solution.py:240
  21.4 4.3 %collective-permute-start.1 = (f32[1,256]{1,0:T(1,128)S(1)}, f32[1,256]{1,0:T(1,128)S(1)}, u32[]{:S(2)}, u32[]{:S(2)}) collective-permute-start(f32[1,256]{1,0:T(1,128)S(1)} %get-tuple-element.14), channel_id=1, source_target_pairs={{1,0},{2,1},{3,2},{4,3},{5,4},{6,5},{7,6},{8,7},{9,8},{10,9},{11,1... | collective-permute-start | bytes 3080 | tf_op jit(solution)/shard_map/ppermute | solution.py:222
  23.3 4.9 %collective-permute-start = (f32[1,256]{1,0:T(1,128)S(1)}, f32[1,256]{1,0:T(1,128)S(1)}, u32[]{:S(2)}, u32[]{:S(2)}) collective-permute-start(f32[1,256]{1,0:T(1,128)S(1)} %get-tuple-element.15), channel_id=1, source_target_pairs={{0,1},{1,2},{2,3},{3,4},{4,5},{5,6},{6,7},{7,8},{8,9},{9,10},{10,1... | collective-permute-start | bytes 3080 | tf_op jit(solution)/shard_map/ppermute | solution.py:222
  28.4 12.4 %collective-permute-start.4 = (bf16[128,256]{1,0:T(8,128)(2,1)S(1)}, bf16[128,256]{1,0:T(8,128)(2,1)S(1)}, u32[]{:S(2)}, u32[]{:S(2)}) collective-permute-start(bf16[128,256]{1,0:T(8,128)(2,1)S(1)} %shard_map.87), channel_id=1, source_target_pairs={{0,6},{1,7},{2,4},{3,5},{4,2},{5,3},{6,0},{7,1},{8,14},{9,15},{10,... | collective-permute-start | bytes 196616 | tf_op jit(solution)/shard_map/ppermute | solution.py:226
  31.8 9.3 %collective-permute-start.3 = (bf16[128,256]{1,0:T(8,128)(2,1)S(1)}, bf16[128,256]{1,0:T(8,128)(2,1)S(1)}, u32[]{:S(2)}, u32[]{:S(2)}) collective-permute-start(bf16[128,256]{1,0:T(8,128)(2,1)S(1)} %shard_map.87), channel_id=1, source_target_pairs={{0,4},{1,5},{2,6},{3,7},{4,0},{5,1},{6,2},{7,3},{8,12},{9,13},{10,... | collective-permute-start | bytes 196616 | tf_op jit(solution)/shard_map/ppermute | solution.py:226
  38.9 6.2 %collective-permute-start.2 = (bf16[128,256]{1,0:T(8,128)(2,1)S(1)}, bf16[128,256]{1,0:T(8,128)(2,1)S(1)}, u32[]{:S(2)}, u32[]{:S(2)}) collective-permute-start(bf16[128,256]{1,0:T(8,128)(2,1)S(1)} %shard_map.87), channel_id=1, source_target_pairs={{0,2},{1,3},{2,0},{3,1},{4,6},{5,7},{6,4},{7,5},{8,10},{9,11},{10,... | collective-permute-start | bytes 196616 | tf_op jit(solution)/shard_map/ppermute | solution.py:226
  45.0 3.6 %copy-start.4 = (s32[4,3]{1,0:T(4,128)S(1)}, s32[4,3]{1,0:T(4,128)}, u32[]{:S(2)}) copy-start(s32[4,3]{1,0:T(4,128)} %list_ref.1) | copy-start | bytes 148
  45.1 3.6 %collective-permute-start.5 = (bf16[4,128,256]{2,1,0:T(8,128)(2,1)S(1)}, bf16[4,128,256]{2,1,0:T(8,128)(2,1)S(1)}, u32[]{:S(2)}, u32[]{:S(2)}) collective-permute-start(bf16[4,128,256]{2,1,0:T(8,128)(2,1)S(1)} %pad_maximum_fusion.mine_ref), channel_id=1, source_target_pairs={{0,1},{1,0},{2,3},{3,2},{4,5},{5,4},{6,7},{7,6},{8,9},{9,8},{10,11... | collective-permute-start | bytes 786440 | tf_op jit(solution)/shard_map/ppermute | solution.py:226
  53.1 12.2 %collective-permute-start.6 = (bf16[272,128]{1,0:T(8,128)(2,1)S(1)}, bf16[272,128]{1,0:T(8,128)(2,1)S(1)}, u32[]{:S(2)}, u32[]{:S(2)}) collective-permute-start(bf16[272,128]{1,0:T(8,128)(2,1)S(1)} %get-tuple-element.12), channel_id=1, source_target_pairs={{0,8},{8,16},{16,24},{24,32},{32,40},{40,48},{48,56},{56,64},{64,7... | collective-permute-start | bytes 208904 | tf_op jit(solution)/shard_map/ppermute | solution.py:222
  63.3 9.5 %collective-permute-start.7 = (bf16[272,128]{1,0:T(8,128)(2,1)S(1)}, bf16[272,128]{1,0:T(8,128)(2,1)S(1)}, u32[]{:S(2)}, u32[]{:S(2)}) collective-permute-start(bf16[272,128]{1,0:T(8,128)(2,1)S(1)} %get-tuple-element.13), channel_id=1, source_target_pairs={{8,0},{16,8},{24,16},{32,24},{40,32},{48,40},{56,48},{64,56},{72,6... | collective-permute-start | bytes 208904 | tf_op jit(solution)/shard_map/ppermute | solution.py:222

commit v2 on v1

--- a/solution.py
+++ b/solution.py
@@ -91,21 +91,27 @@
         out_ref[g * GROUP : (g + 1) * GROUP, :] = (dot(pick, products) + dot(place, meta)).astype(BF16)
 
 
-def shade_kernel(z_ref, before_ref, after_ref, out_ref):
-    z = z_ref[...]
-    shape = z.shape
-    row, col = iota(shape, 0), iota(shape, 1)
-    up = jnp.where(row == 0, before_ref[...], pltpu.roll(z, 1, 0))
-    down = jnp.where(row == shape[0] - 1, after_ref[...], pltpu.roll(z, shape[0] - 1, 0))
+def shade_of(z, up, down):
+    col = iota(z.shape, 1)
     left = jnp.where(col == 0, F32(0), pltpu.roll(z, 1, 1))
-    right = jnp.where(col == shape[1] - 1, F32(0), pltpu.roll(z, shape[1] - 1, 1))
+    right = jnp.where(col == z.shape[1] - 1, F32(0), pltpu.roll(z, z.shape[1] - 1, 1))
     grad_y = (down - up) * 0.5
     grad_x = (right - left) * 0.5
-    shade = (0.8660254 - 0.4 * grad_x - 0.3 * grad_y) / jnp.sqrt(1.0 + grad_x * grad_x + grad_y * grad_y)
-    out_ref[...] = shade.astype(BF16)
-
-
-def main_kernel(recv_ref, mine_ref, theirs_ref, list_ref, out_ref, part_ref, up_ref, down_ref, across_ref, meta_ref):
+    return (0.8660254 - 0.4 * grad_x - 0.3 * grad_y) / jnp.sqrt(1.0 + grad_x * grad_x + grad_y * grad_y)
+
+
+def shade_kernel(z_ref, beside_ref, out_ref):
+    z = z_ref[...]
+    out_ref[:ROWS, :] = shade_of(z, pltpu.roll(z, 1, 0), pltpu.roll(z, ROWS - 1, 0)).astype(BF16)
+    row = iota((8, TILE), 0)
+    border = jnp.where(row < 2, z[:8], jnp.where(row < 4, pltpu.roll(z[ROWS - 8 :], 4, 0), F32(0)))
+    edge = jnp.where(lax.axis_index("bands") == 0, beside_ref[:1], beside_ref[ROWS - 1 :])
+    border = jnp.where(row == 4, edge, border)
+    high = border.astype(BF16).astype(F32)
+    out_ref[ROWS:, :] = jnp.concatenate([high, border - high], axis=0).astype(BF16)
+
+
+def resample_kernel(recv_ref, out_ref, across_ref, meta_ref):
     row, col = iota((GROUP, GROUP), 0), iota((GROUP, GROUP), 1)
     slot = row & 63
     target = jnp.where(
@@ -136,18 +142,7 @@
         here = jnp.where(diff == tap, fields[2 + tap], here)
         after = jnp.where(diff + 16 == tap, fields[2 + tap], after)
     block = jnp.broadcast_to(block, (16, slots))
-
-    tile_me = lax.axis_index("tile")
-    band_me = lax.axis_index("bands")
-    core_me, x_me = lax.rem(band_me, 2), lax.div(band_me, 2)
-    rows_of = ones_where(iota((HALF, TILE), 0) == (iota((HALF, TILE), 1) >> 1)).astype(BF16)
-    cols_of = ones_where((iota((TILE, HALF), 0) >> 1) == iota((TILE, HALF), 1)).astype(BF16)
-    part_ref[...] = jnp.zeros(part_ref.shape, F32)
-    up_ref[...] = jnp.zeros(up_ref.shape, BF16)
-    down_ref[...] = jnp.zeros(down_ref.shape, BF16)
     across = across_ref[...]
-    counts = [jnp.int32(0), jnp.int32(0)]
-    codes = [[jnp.int32(0), jnp.int32(0)], [jnp.int32(0), jnp.int32(0)]]
     for tile in range(TILES):
         weights = jnp.concatenate(
             [
@@ -156,31 +151,81 @@
             ],
             axis=0,
         )
-        resampled = dot(weights, across)
-        mine = mine_ref[tile ^ x_me].astype(F32)
-        theirs = theirs_ref[tile ^ x_me].astype(F32)
-        top = jnp.where(core_me == 0, mine, theirs)
-        bottom = jnp.where(core_me == 0, theirs, mine)
-        finished = (resampled * jnp.concatenate([top, bottom], axis=0)).astype(BF16)
-        out_ref[tile * TILE : (tile + 1) * TILE, :] = finished
-        pairs = dot(rows_of, finished)
-        high = pairs.astype(BF16)
-        low = (pairs - high.astype(F32)).astype(BF16)
-        reduced = (dot(high, cols_of) + dot(low, cols_of)) * 0.25
+        out_ref[tile * TILE : (tile + 1) * TILE, :] = dot(weights, across)
+
+
+def finish_kernel(
+    resampled_ref,
+    mine_ref,
+    theirs_ref,
+    list_ref,
+    out_ref,
+    part_ref,
+    up_ref,
+    down_ref,
+    border_ref,
+    reduced_ref,
+    column_ref,
+    stage_ref,
+    sems,
+):
+    tile_me = lax.axis_index("tile")
+    band_me = lax.axis_index("bands")
+    core_me, x_me = lax.rem(band_me, 2), lax.div(band_me, 2)
+
+    def two_blocks(tile, rows):
+        mine = mine_ref[tile ^ x_me, rows, :].astype(F32)
+        theirs = theirs_ref[tile ^ x_me, rows, :].astype(F32)
+        return jnp.where(core_me == 0, mine, theirs), jnp.where(core_me == 0, theirs, mine)
+
+    for tile in range(TILES):
+        for i, part in enumerate(two_blocks(tile, slice(ROWS, ROWS + 16))):
+            exact = part[:8] + part[8:]
+            for f in range(5):
+                border_ref[f, 2 * tile + i : 2 * tile + i + 1, :] = exact[f : f + 1]
+    first, second, before_last, last, edge = [border_ref[f] for f in range(5)]
+    row = iota((8, TILE), 0)
+    first_shade = shade_of(first, jnp.where(row == 0, edge[7:8], pltpu.roll(last, 1, 0)), second)
+    last_shade = shade_of(last, before_last, jnp.where(row == 7, edge[0:1], pltpu.roll(first, 7, 0)))
+
+    cols_of = ones_where((iota((TILE, HALF), 0) >> 1) == iota((TILE, HALF), 1)).astype(BF16)
+    copies = []
+    for tile in range(TILES):
+        shade = []
+        for i, block in enumerate(two_blocks(tile, slice(0, ROWS))):
+            b = 2 * tile + i
+            shade.append(jnp.where(row == 0, first_shade[b : b + 1], block[:8]))
+            shade.append(block[8:-8])
+            shade.append(jnp.where(row == 7, last_shade[b : b + 1], block[-8:]))
+        rows = slice(tile * TILE, (tile + 1) * TILE)
+        finished = (resampled_ref[rows, :] * jnp.concatenate(shade, axis=0)).astype(BF16)
+        stage_ref[rows, :] = finished
+        copy = pltpu.make_async_copy(stage_ref.at[rows], out_ref.at[rows], sems.at[tile])
+        copy.start()
+        copies.append(copy)
+        column_ref[...] = dot(finished, cols_of)
+        reduced_ref[tile] = (column_ref[pl.ds(0, HALF, stride=2), :] + column_ref[pl.ds(1, HALF, stride=2), :]) * 0.25
+
+    part_ref[...] = jnp.zeros(part_ref.shape, F32)
+    up_ref[...] = jnp.zeros(up_ref.shape, BF16)
+    down_ref[...] = jnp.zeros(down_ref.shape, BF16)
+    counts = [jnp.int32(0), jnp.int32(0)]
+    codes = [[jnp.int32(0), jnp.int32(0)], [jnp.int32(0), jnp.int32(0)]]
+    for tile in range(TILES):
         offset = list_ref[tile, 0] - tile_me
         code = list_ref[tile, 1] * 4 + list_ref[tile, 2]
 
         @pl.when(offset == 0)
-        def _(reduced=reduced, code=code):
-            part_ref[code] = part_ref[code] + reduced
+        def _(tile=tile, code=code):
+            part_ref[code] = part_ref[code] + reduced_ref[tile]
 
         for way, (step, ref) in enumerate(((1, up_ref), (-1, down_ref))):
             goes = offset == step
             rank = jnp.minimum(counts[way], 1)
 
             @pl.when(goes)
-            def _(reduced=reduced, rank=rank, ref=ref):
-                ref[pl.ds(pl.multiple_of(rank * HALF, HALF), HALF), :] = reduced.astype(BF16)
+            def _(tile=tile, rank=rank, ref=ref):
+                ref[pl.ds(pl.multiple_of(rank * HALF, HALF), HALF), :] = reduced_ref[tile].astype(BF16)
 
             for s in range(2):
                 codes[way][s] = jnp.where(goes & (rank == s), code + 1, codes[way][s])
@@ -188,6 +233,8 @@
     eighth = iota((16, HALF), 0) < 8
     for way, ref in enumerate((up_ref, down_ref)):
         ref[2 * HALF :, :] = jnp.where(eighth, codes[way][0], codes[way][1]).astype(F32).astype(BF16)
+    for copy in copies:
+        copy.wait()
 
 
 def combine_kernel(part_ref, up_ref, down_ref, out_ref):
@@ -205,14 +252,14 @@
         out_ref[level, top : top + HALF, left : left + HALF] = total.astype(BF16)
 
 
-def call(kernel, outs, ins, scratch=(), cost=None):
+def call(kernel, outs, ins, scratch=(), cost=None, params=PARAMS, out_specs=None):
     return pl.pallas_call(
         kernel,
         out_shape=outs,
         in_specs=ins,
-        out_specs=jax.tree.map(lambda _: VMEM, outs),
+        out_specs=out_specs or jax.tree.map(lambda _: VMEM, outs),
         scratch_shapes=scratch,
-        compiler_params=PARAMS,
+        compiler_params=params,
         cost_estimate=cost,
     )
 
@@ -228,27 +275,34 @@
 
 def shards(scene_rows, row_dest, row_pos, along_taps, across_taps, elevation, pyramid_list):
     shape = jax.ShapeDtypeStruct
-    outgoing = call(prep_kernel, shape((OWNERS * CHUNK, HALF), BF16), [VMEM] * 5)(
+    outgoing = call(prep_kernel, shape((OWNERS * CHUNK, HALF), BF16), [VMEM] * 5, params=pltpu.CompilerParams(vmem_limit_bytes=60 * 1024 * 1024))(
         scene_rows[0],
         row_dest.T,
         row_pos.T,
         along_taps.transpose(1, 2, 0),
         across_taps[0].T,
     )
-    outgoing, elevation = lax.optimization_barrier((outgoing, elevation))
+    both, last = ("tile", "bands"), lax.axis_size("bands") - 1
+    owners = [last * t + t for t in range(lax.axis_size("tile"))]
+    pairs = list(zip(owners[1:], owners[:-1])) + [(i + last, j + last) for i, j in zip(owners[:-1], owners[1:])]
+    beside = lax.ppermute(elevation, both, pairs)
+    outgoing, beside = lax.optimization_barrier((outgoing, beside))
     units = outgoing.reshape(OWNERS * CHUNK // 2, 2, HALF)
     received = lax.all_to_all(units, "tile", split_axis=0, concat_axis=0, tiled=True)
     received = received.reshape(OWNERS * CHUNK, HALF)
 
-    both = ("tile", "bands")
-    before = shift(elevation[ROWS - 1 :], both, 1)
-    after = shift(elevation[:1], both, -1)
-    shade = call(shade_kernel, shape((ROWS, TILE), BF16), [VMEM] * 3)(elevation, before, after)
+    shade = call(shade_kernel, shape((ROWS + 16, TILE), BF16), [VMEM] * 2)(elevation, beside)
     mine = jnp.stack([shade, exchange(shade, 2), exchange(shade, 4), exchange(shade, 6)])
     theirs = exchange(mine, 1)
-
+    resampled = call(
+        resample_kernel,
+        shape((TILES * TILE, TILE), F32),
+        [VMEM],
+        [pltpu.VMEM((OWNERS * CAP, TILE), BF16), pltpu.VMEM((OWNERS, HALF), F32)],
+        pl.CostEstimate(flops=400_000_000, bytes_accessed=1_500_000, transcendentals=0),
+    )(received)
     finished, part, up, down = call(
-        main_kernel,
+        finish_kernel,
         (
             shape((TILES * TILE, TILE), BF16),
             shape((8, HALF, HALF), F32),
@@ -256,8 +310,15 @@
             shape((PAYLOAD, HALF), BF16),
         ),
         [VMEM, VMEM, VMEM, SMEM],
-        [pltpu.VMEM((OWNERS * CAP, TILE), BF16), pltpu.VMEM((OWNERS, HALF), F32)],
-    )(received, mine, theirs, pyramid_list)
+        [
+            pltpu.VMEM((5, 8, TILE), F32),
+            pltpu.VMEM((TILES, HALF, HALF), F32),
+            pltpu.VMEM((TILE, HALF), F32),
+            pltpu.VMEM((TILES * TILE, TILE), BF16),
+            pltpu.SemaphoreType.DMA((TILES,)),
+        ],
+        out_specs=(pl.BlockSpec(memory_space=pl.ANY), VMEM, VMEM, VMEM),
+    )(resampled, mine, theirs, pyramid_list)
     pyramid = call(combine_kernel, shape((2, TILE, TILE), BF16), [VMEM] * 3)(
         part, shift(up, "tile", 1), shift(down, "tile", -1)
     )

time: 74.2 us -> 62.5 us (0.84)
  the two profiles are of different devices: /device:TPU:122 before, /device:TPU:24 now
where the time goes in v2:
time: 62.5 us; the launch traced here: 62.1 us
  starting transfers between devices  38.7 us (62%)
  waiting for transfers between devices  16.1 us (26%)
  Pallas kernels  6.48 us (10%)
  between operations  0.76 us (1%)
    all_to_all x1, starting transfers between devices, shards(): lax.all_to_all(units, 'tile', split_axis=0, concat_axis=0, tiled=True)  18.5 us
    ppermute x4, starting transfers between devices, exchange(): lax.ppermute(value, 'bands', [(i, i ^ mask) for i in range(lax.axis_size(...  11.7 us
    ppermute x2, waiting for transfers between devices, shift(): lax.ppermute(value, axes, [(i, i + by) for i in range(size) if 0 <= i + b...  6.38 us
    ppermute x2, starting transfers between devices, shift(): lax.ppermute(value, axes, [(i, i + by) for i in range(size) if 0 <= i + b...  5.87 us
    ppermute x1, waiting for transfers between devices, shards(): beside = lax.ppermute(elevation, both, pairs)  3.77 us
    all_to_all x1, waiting for transfers between devices, shards(): lax.all_to_all(units, 'tile', split_axis=0, concat_axis=0, tiled=True)  3.64 us
    pallas_call x1, Pallas kernels, shards(): call(prep_kernel, shape((OWNERS * CHUNK, HALF), BF16), [VMEM] * 5, params...  2.75 us
    ppermute x1, starting transfers between devices, shards(): beside = lax.ppermute(elevation, both, pairs)  2.65 us
  transfers between devices with their start and end apart: 8, of which 6 were waited for; matrix products, arithmetic and copies ran while one was open for 0% of the time, Pallas kernels for 6%

profile of v2, /device:TPU:24, one launch (start us, length us, event | category | flops | bytes accessed | tf_op | source)
XLA Modules:
  0.0 62.1 jit_solution(786484783177444204)
XLA Ops:
  0.6 2.7 %collective-permute-start = (f32[128,256]{1,0:T(8,128)}, f32[128,256]{1,0:T(8,128)S(1)}, u32[]{:S(2)}, u32[]{:S(2)}) collective-permute-start(f32[128,256]{1,0:T(8,128)} %z_ref.1), channel_id=1, source_target_pairs={{8,0},{16,8},{24,16},{32,24},{40,32},{48,40},{56,48},{64,56},{72,6... | collective-permute-start | bytes 393224 | tf_op jit(solution)/shard_map/ppermute | solution.py:288
  3.3 2.8 %shard_map.86 = bf16[1152,128]{1,0:T(8,128)(2,1)} custom-call(bf16[128,768]{1,0:T(8,128)(2,1)} %bitcast.19, s32[2,128]{1,0:T(2,128)} %bitcast.25, s32[2,128]{1,0:T(2,128)} %bitcast.26, bf16[2,4,128]{2,1,0:T(4,128)(2,1)} %bitcast.24, bf16[8,256]{1,0:T(8,128)(2,1)} %bitcast.23), custom_call_target="tpu_custom_call" | custom-call | tf_op jit(solution)/shard_map/pallas_call | solution.py:278
  6.0 3.8 %collective-permute-done.beside_ref = f32[128,256]{1,0:T(8,128)S(1)} collective-permute-done((f32[128,256]{1,0:T(8,128)}, f32[128,256]{1,0:T(8,128)S(1)}, u32[]{:S(2)}, u32[]{:S(2)}) %collective-permute-start) | collective-permute-done | bytes 131104 | tf_op jit(solution)/shard_map/ppermute | solution.py:288
  9.8 0.0 copy-start
  9.8 18.5 %all-to-all-start = ((bf16[576,2,128]{2,1,0:T(2,128)(2,1)}), bf16[576,2,128]{2,1,0:T(2,128)(2,1)S(1)}, u32[]{:S(2)}, u32[]{:S(2)}) async-start(bf16[576,2,128]{2,1,0:T(2,128)(2,1)} %bitcast.17), calls=%async_computation | async-start | bytes 589824 | tf_op jit(solution)/shard_map/all_to_all | solution.py:291
  28.3 0.0 copy-done
  28.3 0.2 shard_map.88
  28.5 1.9 %collective-permute-start.3 = (bf16[144,256]{1,0:T(8,128)(2,1)S(1)}, bf16[144,256]{1,0:T(8,128)(2,1)S(1)}, u32[]{:S(2)}, u32[]{:S(2)}) collective-permute-start(bf16[144,256]{1,0:T(8,128)(2,1)S(1)} %shard_map.88), channel_id=1, source_target_pairs={{0,6},{1,7},{2,4},{3,5},{4,2},{5,3},{6,0},{7,1},{8,14},{9,15},{10,... | collective-permute-start | bytes 221192 | tf_op jit(solution)/shard_map/ppermute | solution.py:273
  30.4 1.9 %collective-permute-start.2 = (bf16[144,256]{1,0:T(8,128)(2,1)S(1)}, bf16[144,256]{1,0:T(8,128)(2,1)S(1)}, u32[]{:S(2)}, u32[]{:S(2)}) collective-permute-start(bf16[144,256]{1,0:T(8,128)(2,1)S(1)} %shard_map.88), channel_id=1, source_target_pairs={{0,4},{1,5},{2,6},{3,7},{4,0},{5,1},{6,2},{7,3},{8,12},{9,13},{10,... | collective-permute-start | bytes 221192 | tf_op jit(solution)/shard_map/ppermute | solution.py:273
  32.4 6.0 %collective-permute-start.1 = (bf16[144,256]{1,0:T(8,128)(2,1)S(1)}, bf16[144,256]{1,0:T(8,128)(2,1)S(1)}, u32[]{:S(2)}, u32[]{:S(2)}) collective-permute-start(bf16[144,256]{1,0:T(8,128)(2,1)S(1)} %shard_map.88), channel_id=1, source_target_pairs={{0,2},{1,3},{2,0},{3,1},{4,6},{5,7},{6,4},{7,5},{8,10},{9,11},{10,... | collective-permute-start | bytes 221192 | tf_op jit(solution)/shard_map/ppermute | solution.py:273
  38.3 0.0 collective-permute-done.3
  38.4 0.3 collective-permute-done.2
  38.7 2.0 %collective-permute-done.1 = bf16[144,256]{1,0:T(8,128)(2,1)S(1)} collective-permute-done((bf16[144,256]{1,0:T(8,128)(2,1)S(1)}, bf16[144,256]{1,0:T(8,128)(2,1)S(1)}, u32[]{:S(2)}, u32[]{:S(2)}) %collective-permute-start.1) | collective-permute-done | bytes 73760 | tf_op jit(solution)/shard_map/ppermute | solution.py:273
  40.7 1.9 %collective-permute-start.4 = (bf16[4,144,256]{2,1,0:T(8,128)(2,1)S(1)}, bf16[4,144,256]{2,1,0:T(8,128)(2,1)S(1)}, u32[]{:S(2)}, u32[]{:S(2)}) collective-permute-start(bf16[4,144,256]{2,1,0:T(8,128)(2,1)S(1)} %pad_maximum_fusion.mine_ref), channel_id=1, source_target_pairs={{0,1},{1,0},{2,3},{3,2},{4,5},{5,4},{6,7},{7,6},{8,9},{9,8},{10,11... | collective-permute-start | bytes 884744 | tf_op jit(solution)/shard_map/ppermute | solution.py:273
  42.6 3.6 %all-to-all-done = bf16[576,2,128]{2,1,0:T(2,128)(2,1)S(1)} async-done(((bf16[576,2,128]{2,1,0:T(2,128)(2,1)}), bf16[576,2,128]{2,1,0:T(2,128)(2,1)S(1)}, u32[]{:S(2)}, u32[]{:S(2)}) %all-to-all-start) | async-done | bytes 294944 | tf_op jit(solution)/shard_map/all_to_all | solution.py:291
  46.3 0.0 copy-start.1
  46.3 1.0 %shard_map.87.resampled_ref = f32[1024,256]{1,0:T(8,128)S(1)} custom-call(bf16[1152,128]{1,0:T(8,128)(2,1)S(1)} %bitcast.16), custom_call_target="tpu_custom_call" | custom-call | flops 400000000 | bytes 1500000 | tf_op jit(solution)/shard_map/pallas_call | solution.py:297
  47.3 0.0 collective-permute-done.4.theirs_ref
  47.3 0.0 copy-done.1
  47.3 1.6 %shard_map.89 = (bf16[1024,256]{1,0:T(8,128)(2,1)}, f32[8,128,128]{2,1,0:T(8,128)S(1)}, bf16[272,128]{1,0:T(8,128)(2,1)S(1)}, bf16[272,128]{1,0:T(8,128)(2,1)S(1)}) custom-call(f32[1024,256]{1,0:T(8,128)S(1)} %shard_map.87.resampled_ref, bf16[4,144,256]{2,1,0:T(8,128)(2,1)S(1)} %pad_maximum_fusion.mine_ref, ...), custom_call_target="tpu_custom_call" | custom-call | tf_op jit(solution)/shard_map/pallas_call | solution.py:304
  48.9 4.0 %collective-permute-start.5 = (bf16[272,128]{1,0:T(8,128)(2,1)S(1)}, bf16[272,128]{1,0:T(8,128)(2,1)S(1)}, u32[]{:S(2)}, u32[]{:S(2)}) collective-permute-start(bf16[272,128]{1,0:T(8,128)(2,1)S(1)} %get-tuple-element.12), channel_id=1, source_target_pairs={{0,8},{8,16},{16,24},{24,32},{32,40},{40,48},{48,56},{56,64},{64,7... | collective-permute-start | bytes 208904 | tf_op jit(solution)/shard_map/ppermute | solution.py:269
  52.9 1.9 %collective-permute-start.6 = (bf16[272,128]{1,0:T(8,128)(2,1)S(1)}, bf16[272,128]{1,0:T(8,128)(2,1)S(1)}, u32[]{:S(2)}, u32[]{:S(2)}) collective-permute-start(bf16[272,128]{1,0:T(8,128)(2,1)S(1)} %get-tuple-element.13), channel_id=1, source_target_pairs={{8,0},{16,8},{24,16},{32,24},{40,32},{48,40},{56,48},{64,56},{72,6... | collective-permute-start | bytes 208904 | tf_op jit(solution)/shard_map/ppermute | solution.py:269
  54.8 0.3 collective-permute-done.5.up_ref
  55.1 6.1 %collective-permute-done.6.down_ref = bf16[272,128]{1,0:T(8,128)(2,1)S(1)} collective-permute-done((bf16[272,128]{1,0:T(8,128)(2,1)S(1)}, bf16[272,128]{1,0:T(8,128)(2,1)S(1)}, u32[]{:S(2)}, u32[]{:S(2)}) %collective-permute-start.6) | collective-permute-done | bytes 69664 | tf_op jit(solution)/shard_map/ppermute | solution.py:269
  61.2 0.9 %shard_map.90 = bf16[2,256,256]{2,1,0:T(8,128)(2,1)} custom-call(f32[8,128,128]{2,1,0:T(8,128)S(1)} %get-tuple-element.11.part_ref, bf16[272,128]{1,0:T(8,128)(2,1)S(1)} %collective-permute-done.5.up_ref, bf16[272,128]{1,0:T(8,128)(2,1)S(1)} %collective-permute-done.6.down_ref), custom_call_target="tpu_custom_call" | custom-call | tf_op jit(solution)/shard_map/pallas_call | solution.py:322
  (1 shorter events, 0.0 us)
Async XLA Ops:
  0.6 9.2 %collective-permute-start = (f32[128,256]{1,0:T(8,128)}, f32[128,256]{1,0:T(8,128)S(1)}, u32[]{:S(2)}, u32[]{:S(2)}) collective-permute-start(f32[128,256]{1,0:T(8,128)} %z_ref.1), channel_id=1, source_target_pairs={{8,0},{16,8},{24,16},{32,24},{40,32},{48,40},{56,48},{64,56},{72,6... | collective-permute-start | bytes 393224 | tf_op jit(solution)/shard_map/ppermute | solution.py:288
  9.8 18.5 %copy-start = (f32[128,256]{1,0:T(8,128)S(1)}, f32[128,256]{1,0:T(8,128)}, u32[]{:S(2)}) copy-start(f32[128,256]{1,0:T(8,128)} %z_ref.1) | copy-start | bytes 393220
  9.8 36.5 %all-to-all-start = ((bf16[576,2,128]{2,1,0:T(2,128)(2,1)}), bf16[576,2,128]{2,1,0:T(2,128)(2,1)S(1)}, u32[]{:S(2)}, u32[]{:S(2)}) async-start(bf16[576,2,128]{2,1,0:T(2,128)(2,1)} %bitcast.17), calls=%async_computation | async-start | bytes 589824 | tf_op jit(solution)/shard_map/all_to_all | solution.py:291
  28.5 9.8 %collective-permute-start.3 = (bf16[144,256]{1,0:T(8,128)(2,1)S(1)}, bf16[144,256]{1,0:T(8,128)(2,1)S(1)}, u32[]{:S(2)}, u32[]{:S(2)}) collective-permute-start(bf16[144,256]{1,0:T(8,128)(2,1)S(1)} %shard_map.88), channel_id=1, source_target_pairs={{0,6},{1,7},{2,4},{3,5},{4,2},{5,3},{6,0},{7,1},{8,14},{9,15},{10,... | collective-permute-start | bytes 221192 | tf_op jit(solution)/shard_map/ppermute | solution.py:273
  30.4 8.2 %collective-permute-start.2 = (bf16[144,256]{1,0:T(8,128)(2,1)S(1)}, bf16[144,256]{1,0:T(8,128)(2,1)S(1)}, u32[]{:S(2)}, u32[]{:S(2)}) collective-permute-start(bf16[144,256]{1,0:T(8,128)(2,1)S(1)} %shard_map.88), channel_id=1, source_target_pairs={{0,4},{1,5},{2,6},{3,7},{4,0},{5,1},{6,2},{7,3},{8,12},{9,13},{10,... | collective-permute-start | bytes 221192 | tf_op jit(solution)/shard_map/ppermute | solution.py:273
  32.4 8.3 %collective-permute-start.1 = (bf16[144,256]{1,0:T(8,128)(2,1)S(1)}, bf16[144,256]{1,0:T(8,128)(2,1)S(1)}, u32[]{:S(2)}, u32[]{:S(2)}) collective-permute-start(bf16[144,256]{1,0:T(8,128)(2,1)S(1)} %shard_map.88), channel_id=1, source_target_pairs={{0,2},{1,3},{2,0},{3,1},{4,6},{5,7},{6,4},{7,5},{8,10},{9,11},{10,... | collective-permute-start | bytes 221192 | tf_op jit(solution)/shard_map/ppermute | solution.py:273
  40.7 6.6 %collective-permute-start.4 = (bf16[4,144,256]{2,1,0:T(8,128)(2,1)S(1)}, bf16[4,144,256]{2,1,0:T(8,128)(2,1)S(1)}, u32[]{:S(2)}, u32[]{:S(2)}) collective-permute-start(bf16[4,144,256]{2,1,0:T(8,128)(2,1)S(1)} %pad_maximum_fusion.mine_ref), channel_id=1, source_target_pairs={{0,1},{1,0},{2,3},{3,2},{4,5},{5,4},{6,7},{7,6},{8,9},{9,8},{10,11... | collective-permute-start | bytes 884744 | tf_op jit(solution)/shard_map/ppermute | solution.py:273
  46.3 1.0 %copy-start.1 = (s32[4,3]{1,0:T(4,128)S(1)}, s32[4,3]{1,0:T(4,128)}, u32[]{:S(2)}) copy-start(s32[4,3]{1,0:T(4,128)} %list_ref.1) | copy-start | bytes 148
  48.9 6.2 %collective-permute-start.5 = (bf16[272,128]{1,0:T(8,128)(2,1)S(1)}, bf16[272,128]{1,0:T(8,128)(2,1)S(1)}, u32[]{:S(2)}, u32[]{:S(2)}) collective-permute-start(bf16[272,128]{1,0:T(8,128)(2,1)S(1)} %get-tuple-element.12), channel_id=1, source_target_pairs={{0,8},{8,16},{16,24},{24,32},{32,40},{40,48},{48,56},{56,64},{64,7... | collective-permute-start | bytes 208904 | tf_op jit(solution)/shard_map/ppermute | solution.py:269
  52.9 8.3 %collective-permute-start.6 = (bf16[272,128]{1,0:T(8,128)(2,1)S(1)}, bf16[272,128]{1,0:T(8,128)(2,1)S(1)}, u32[]{:S(2)}, u32[]{:S(2)}) collective-permute-start(bf16[272,128]{1,0:T(8,128)(2,1)S(1)} %get-tuple-element.13), channel_id=1, source_target_pairs={{8,0},{16,8},{24,16},{32,24},{40,32},{48,40},{56,48},{64,56},{72,6... | collective-permute-start | bytes 208904 | tf_op jit(solution)/shard_map/ppermute | solution.py:269

commit v3 on v2

--- a/solution.py
+++ b/solution.py
@@ -24,6 +24,9 @@
 VMEM = pl.BlockSpec(memory_space=pltpu.VMEM)
 SMEM = pl.BlockSpec(memory_space=pltpu.SMEM)
 PARAMS = pltpu.CompilerParams(vmem_limit_bytes=24 * 1024 * 1024)
+
+
+WINDOW = pl.CostEstimate(flops=60_000_000_000, bytes_accessed=1_000_000, transcendentals=0)
 
 
 def iota(shape, axis):
@@ -161,8 +164,8 @@
     list_ref,
     out_ref,
     part_ref,
-    up_ref,
-    down_ref,
+    far_ref,
+    near_ref,
     border_ref,
     reduced_ref,
     column_ref,
@@ -207,8 +210,9 @@
         reduced_ref[tile] = (column_ref[pl.ds(0, HALF, stride=2), :] + column_ref[pl.ds(1, HALF, stride=2), :]) * 0.25
 
     part_ref[...] = jnp.zeros(part_ref.shape, F32)
-    up_ref[...] = jnp.zeros(up_ref.shape, BF16)
-    down_ref[...] = jnp.zeros(down_ref.shape, BF16)
+    near_ref[...] = jnp.zeros(near_ref.shape, BF16)
+    far_ref[...] = jnp.zeros(far_ref.shape, BF16)
+    side = 1 - 2 * lax.rem(tile_me, 2)
     counts = [jnp.int32(0), jnp.int32(0)]
     codes = [[jnp.int32(0), jnp.int32(0)], [jnp.int32(0), jnp.int32(0)]]
     for tile in range(TILES):
@@ -219,7 +223,7 @@
         def _(tile=tile, code=code):
             part_ref[code] = part_ref[code] + reduced_ref[tile]
 
-        for way, (step, ref) in enumerate(((1, up_ref), (-1, down_ref))):
+        for way, (step, ref) in enumerate(((side, near_ref), (-side, far_ref))):
             goes = offset == step
             rank = jnp.minimum(counts[way], 1)
 
@@ -231,15 +235,15 @@
                 codes[way][s] = jnp.where(goes & (rank == s), code + 1, codes[way][s])
             counts[way] = counts[way] + goes.astype(I32)
     eighth = iota((16, HALF), 0) < 8
-    for way, ref in enumerate((up_ref, down_ref)):
+    for way, ref in enumerate((near_ref, far_ref)):
         ref[2 * HALF :, :] = jnp.where(eighth, codes[way][0], codes[way][1]).astype(F32).astype(BF16)
     for copy in copies:
         copy.wait()
 
 
-def combine_kernel(part_ref, up_ref, down_ref, out_ref):
+def combine_kernel(part_ref, far_ref, near_ref, out_ref):
     arrived = []
-    for ref in (up_ref, down_ref):
+    for ref in (far_ref, near_ref):
         codes = ref[2 * HALF :, :].astype(F32)
         for s in range(2):
             arrived.append((codes[8 * s : 8 * s + 1], ref[s * HALF : (s + 1) * HALF, :].astype(F32)))
@@ -264,9 +268,9 @@
     )
 
 
-def shift(value, axes, by):
-    size = lax.axis_size(axes)
-    return lax.ppermute(value, axes, [(i, i + by) for i in range(size) if 0 <= i + by < size])
+def swap(value, first):
+    pairs = [(i, i + 1) for i in range(first, lax.axis_size("tile") - 1, 2)]
+    return lax.ppermute(value, "tile", pairs + [(j, i) for i, j in pairs])
 
 
 def exchange(value, mask):
@@ -286,12 +290,12 @@
     owners = [last * t + t for t in range(lax.axis_size("tile"))]
     pairs = list(zip(owners[1:], owners[:-1])) + [(i + last, j + last) for i, j in zip(owners[:-1], owners[1:])]
     beside = lax.ppermute(elevation, both, pairs)
-    outgoing, beside = lax.optimization_barrier((outgoing, beside))
+    outgoing, elevation = lax.optimization_barrier((outgoing, elevation))
     units = outgoing.reshape(OWNERS * CHUNK // 2, 2, HALF)
     received = lax.all_to_all(units, "tile", split_axis=0, concat_axis=0, tiled=True)
     received = received.reshape(OWNERS * CHUNK, HALF)
 
-    shade = call(shade_kernel, shape((ROWS + 16, TILE), BF16), [VMEM] * 2)(elevation, beside)
+    shade = call(shade_kernel, shape((ROWS + 16, TILE), BF16), [VMEM] * 2, cost=WINDOW)(elevation, beside)
     mine = jnp.stack([shade, exchange(shade, 2), exchange(shade, 4), exchange(shade, 6)])
     theirs = exchange(mine, 1)
     resampled = call(
@@ -301,7 +305,7 @@
         [pltpu.VMEM((OWNERS * CAP, TILE), BF16), pltpu.VMEM((OWNERS, HALF), F32)],
         pl.CostEstimate(flops=400_000_000, bytes_accessed=1_500_000, transcendentals=0),
     )(received)
-    finished, part, up, down = call(
+    finished, part, far, near = call(
         finish_kernel,
         (
             shape((TILES * TILE, TILE), BF16),
@@ -319,9 +323,8 @@
         ],
         out_specs=(pl.BlockSpec(memory_space=pl.ANY), VMEM, VMEM, VMEM),
     )(resampled, mine, theirs, pyramid_list)
-    pyramid = call(combine_kernel, shape((2, TILE, TILE), BF16), [VMEM] * 3)(
-        part, shift(up, "tile", 1), shift(down, "tile", -1)
-    )
+    far, near = swap(far, 1), swap(near, 0)
+    pyramid = call(combine_kernel, shape((2, TILE, TILE), BF16), [VMEM] * 3)(part, far, near)
     return (finished[None], pyramid[None])
 
 

time: 62.5 us -> 61.1 us (0.978)
  the two profiles are of different devices: /device:TPU:24 before, /device:TPU:38 now
where the time goes in v3:
time: 61.1 us; the launch traced here: 60.7 us
  starting transfers between devices  38.8 us (64%)
  waiting for transfers between devices  14.7 us (24%)
  Pallas kernels  6.48 us (11%)
  between operations  0.76 us (1%)
    all_to_all x1, starting transfers between devices, shards(): lax.all_to_all(units, 'tile', split_axis=0, concat_axis=0, tiled=True)  18.5 us
    ppermute x4, starting transfers between devices, exchange(): lax.ppermute(value, 'bands', [(i, i ^ mask) for i in range(lax.axis_size(...  11.7 us
    ppermute x2, starting transfers between devices, swap(): return lax.ppermute(value, 'tile', pairs + [(j, i) for i, j in pairs])  7.84 us
    all_to_all x1, waiting for transfers between devices, shards(): lax.all_to_all(units, 'tile', split_axis=0, concat_axis=0, tiled=True)  7.01 us
    ppermute x2, waiting for transfers between devices, swap(): return lax.ppermute(value, 'tile', pairs + [(j, i) for i, j in pairs])  4.27 us
    ppermute x4, waiting for transfers between devices, exchange(): lax.ppermute(value, 'bands', [(i, i ^ mask) for i in range(lax.axis_size(...  3.37 us
    pallas_call x1, Pallas kernels, shards(): call(prep_kernel, shape((OWNERS * CHUNK, HALF), BF16), [VMEM] * 5, params...  2.75 us
    pallas_call x1, Pallas kernels, shards(): call(finish_kernel, (shape((TILES * TILE, TILE), BF16), shape((8, HALF, H...  1.62 us
  transfers between devices with their start and end apart: 8, of which 5 were waited for; matrix products, arithmetic and copies ran while one was open for 0% of the time, Pallas kernels for 7%

profile of v3, /device:TPU:38, one launch (start us, length us, event | category | flops | bytes accessed | tf_op | source)
XLA Modules:
  0.0 60.7 jit_solution(17017647126652891267)
XLA Ops:
  0.6 0.7 %collective-permute-start = (f32[128,256]{1,0:T(8,128)}, f32[128,256]{1,0:T(8,128)S(1)}, u32[]{:S(2)}, u32[]{:S(2)}) collective-permute-start(f32[128,256]{1,0:T(8,128)} %z_ref), channel_id=1, source_target_pairs={{8,0},{16,8},{24,16},{32,24},{40,32},{48,40},{56,48},{64,56},{72,6... | collective-permute-start | bytes 393224 | tf_op jit(solution)/shard_map/ppermute | solution.py:292
  1.3 2.8 %shard_map.86 = bf16[1152,128]{1,0:T(8,128)(2,1)} custom-call(bf16[128,768]{1,0:T(8,128)(2,1)} %bitcast.19, s32[2,128]{1,0:T(2,128)} %bitcast.25, s32[2,128]{1,0:T(2,128)} %bitcast.26, bf16[2,4,128]{2,1,0:T(4,128)(2,1)} %bitcast.24, bf16[8,256]{1,0:T(8,128)(2,1)} %bitcast.23), custom_call_target="tpu_custom_call" | custom-call | tf_op jit(solution)/shard_map/pallas_call | solution.py:282
  4.1 0.0 copy-start.1
  4.1 18.5 %all-to-all-start = ((bf16[576,2,128]{2,1,0:T(2,128)(2,1)}), bf16[576,2,128]{2,1,0:T(2,128)(2,1)S(1)}, u32[]{:S(2)}, u32[]{:S(2)}) async-start(bf16[576,2,128]{2,1,0:T(2,128)(2,1)} %bitcast.17), calls=%async_computation | async-start | bytes 589824 | tf_op jit(solution)/shard_map/all_to_all | solution.py:295
  22.6 0.0 collective-permute-done.beside_ref
  22.6 0.0 copy-done.1
  22.6 0.2 shard_map.88
  22.8 4.2 %collective-permute-start.3 = (bf16[144,256]{1,0:T(8,128)(2,1)S(1)}, bf16[144,256]{1,0:T(8,128)(2,1)S(1)}, u32[]{:S(2)}, u32[]{:S(2)}) collective-permute-start(bf16[144,256]{1,0:T(8,128)(2,1)S(1)} %shard_map.88), channel_id=1, source_target_pairs={{0,6},{1,7},{2,4},{3,5},{4,2},{5,3},{6,0},{7,1},{8,14},{9,15},{10,... | collective-permute-start | bytes 221192 | tf_op jit(solution)/shard_map/ppermute | solution.py:277
  27.0 2.5 %collective-permute-start.2 = (bf16[144,256]{1,0:T(8,128)(2,1)S(1)}, bf16[144,256]{1,0:T(8,128)(2,1)S(1)}, u32[]{:S(2)}, u32[]{:S(2)}) collective-permute-start(bf16[144,256]{1,0:T(8,128)(2,1)S(1)} %shard_map.88), channel_id=1, source_target_pairs={{0,4},{1,5},{2,6},{3,7},{4,0},{5,1},{6,2},{7,3},{8,12},{9,13},{10,... | collective-permute-start | bytes 221192 | tf_op jit(solution)/shard_map/ppermute | solution.py:277
  29.6 3.1 %collective-permute-start.1 = (bf16[144,256]{1,0:T(8,128)(2,1)S(1)}, bf16[144,256]{1,0:T(8,128)(2,1)S(1)}, u32[]{:S(2)}, u32[]{:S(2)}) collective-permute-start(bf16[144,256]{1,0:T(8,128)(2,1)S(1)} %shard_map.88), channel_id=1, source_target_pairs={{0,2},{1,3},{2,0},{3,1},{4,6},{5,7},{6,4},{7,5},{8,10},{9,11},{10,... | collective-permute-start | bytes 221192 | tf_op jit(solution)/shard_map/ppermute | solution.py:277
  32.7 0.0 collective-permute-done.3
  32.7 2.1 %collective-permute-done.2 = bf16[144,256]{1,0:T(8,128)(2,1)S(1)} collective-permute-done((bf16[144,256]{1,0:T(8,128)(2,1)S(1)}, bf16[144,256]{1,0:T(8,128)(2,1)S(1)}, u32[]{:S(2)}, u32[]{:S(2)}) %collective-permute-start.2) | collective-permute-done | bytes 73760 | tf_op jit(solution)/shard_map/ppermute | solution.py:277
  34.8 1.3 %collective-permute-done.1 = bf16[144,256]{1,0:T(8,128)(2,1)S(1)} collective-permute-done((bf16[144,256]{1,0:T(8,128)(2,1)S(1)}, bf16[144,256]{1,0:T(8,128)(2,1)S(1)}, u32[]{:S(2)}, u32[]{:S(2)}) %collective-permute-start.1) | collective-permute-done | bytes 73760 | tf_op jit(solution)/shard_map/ppermute | solution.py:277
  36.1 1.9 %collective-permute-start.4 = (bf16[4,144,256]{2,1,0:T(8,128)(2,1)S(1)}, bf16[4,144,256]{2,1,0:T(8,128)(2,1)S(1)}, u32[]{:S(2)}, u32[]{:S(2)}) collective-permute-start(bf16[4,144,256]{2,1,0:T(8,128)(2,1)S(1)} %pad_maximum_fusion.mine_ref), channel_id=1, source_target_pairs={{0,1},{1,0},{2,3},{3,2},{4,5},{5,4},{6,7},{7,6},{8,9},{9,8},{10,11... | collective-permute-start | bytes 884744 | tf_op jit(solution)/shard_map/ppermute | solution.py:277
  38.0 7.0 %all-to-all-done = bf16[576,2,128]{2,1,0:T(2,128)(2,1)S(1)} async-done(((bf16[576,2,128]{2,1,0:T(2,128)(2,1)}), bf16[576,2,128]{2,1,0:T(2,128)(2,1)S(1)}, u32[]{:S(2)}, u32[]{:S(2)}) %all-to-all-start) | async-done | bytes 294944 | tf_op jit(solution)/shard_map/all_to_all | solution.py:295
  45.0 0.0 copy-start
  45.0 1.0 %shard_map.87.resampled_ref = f32[1024,256]{1,0:T(8,128)S(1)} custom-call(bf16[1152,128]{1,0:T(8,128)(2,1)S(1)} %bitcast.15), custom_call_target="tpu_custom_call" | custom-call | flops 400000000 | bytes 1500000 | tf_op jit(solution)/shard_map/pallas_call | solution.py:301
  46.0 0.0 collective-permute-done.4.theirs_ref
  46.1 0.0 copy-done
  46.1 1.6 %shard_map.89 = (bf16[1024,256]{1,0:T(8,128)(2,1)}, f32[8,128,128]{2,1,0:T(8,128)S(1)}, bf16[272,128]{1,0:T(8,128)(2,1)S(1)}, bf16[272,128]{1,0:T(8,128)(2,1)S(1)}) custom-call(f32[1024,256]{1,0:T(8,128)S(1)} %shard_map.87.resampled_ref, bf16[4,144,256]{2,1,0:T(8,128)(2,1)S(1)} %pad_maximum_fusion.mine_ref, ...), custom_call_target="tpu_custom_call" | custom-call | tf_op jit(solution)/shard_map/pallas_call | solution.py:308
  47.7 5.9 %collective-permute-start.5 = (bf16[272,128]{1,0:T(8,128)(2,1)S(1)}, bf16[272,128]{1,0:T(8,128)(2,1)S(1)}, u32[]{:S(2)}, u32[]{:S(2)}) collective-permute-start(bf16[272,128]{1,0:T(8,128)(2,1)S(1)} %get-tuple-element.12), channel_id=1, source_target_pairs={{8,16},{24,32},{40,48},{56,64},{72,80},{88,96},{104,112},{120,128}... | collective-permute-start | bytes 208904 | tf_op jit(solution)/shard_map/ppermute | solution.py:273
  53.6 1.9 %collective-permute-start.6 = (bf16[272,128]{1,0:T(8,128)(2,1)S(1)}, bf16[272,128]{1,0:T(8,128)(2,1)S(1)}, u32[]{:S(2)}, u32[]{:S(2)}) collective-permute-start(bf16[272,128]{1,0:T(8,128)(2,1)S(1)} %get-tuple-element.13), channel_id=1, source_target_pairs={{0,8},{16,24},{32,40},{48,56},{64,72},{80,88},{96,104},{112,120},{... | collective-permute-start | bytes 208904 | tf_op jit(solution)/shard_map/ppermute | solution.py:273
  55.6 0.5 collective-permute-done.5.far_ref
  56.0 3.8 %collective-permute-done.6.near_ref = bf16[272,128]{1,0:T(8,128)(2,1)S(1)} collective-permute-done((bf16[272,128]{1,0:T(8,128)(2,1)S(1)}, bf16[272,128]{1,0:T(8,128)(2,1)S(1)}, u32[]{:S(2)}, u32[]{:S(2)}) %collective-permute-start.6) | collective-permute-done | bytes 69664 | tf_op jit(solution)/shard_map/ppermute | solution.py:273
  59.8 0.9 %shard_map.90 = bf16[2,256,256]{2,1,0:T(8,128)(2,1)} custom-call(f32[8,128,128]{2,1,0:T(8,128)S(1)} %get-tuple-element.11.part_ref, bf16[272,128]{1,0:T(8,128)(2,1)S(1)} %collective-permute-done.5.far_ref, bf16[272,128]{1,0:T(8,128)(2,1)S(1)} %collective-permute-done.6.near_ref), custom_call_target="tpu_custom_call" | custom-call | tf_op jit(solution)/shard_map/pallas_call | solution.py:327
  (1 shorter events, 0.0 us)
Async XLA Ops:
  0.6 22.0 %collective-permute-start = (f32[128,256]{1,0:T(8,128)}, f32[128,256]{1,0:T(8,128)S(1)}, u32[]{:S(2)}, u32[]{:S(2)}) collective-permute-start(f32[128,256]{1,0:T(8,128)} %z_ref), channel_id=1, source_target_pairs={{8,0},{16,8},{24,16},{32,24},{40,32},{48,40},{56,48},{64,56},{72,6... | collective-permute-start | bytes 393224 | tf_op jit(solution)/shard_map/ppermute | solution.py:292
  4.1 18.5 %copy-start.1 = (f32[128,256]{1,0:T(8,128)S(1)}, f32[128,256]{1,0:T(8,128)}, u32[]{:S(2)}) copy-start(f32[128,256]{1,0:T(8,128)} %z_ref) | copy-start | bytes 393220
  4.1 41.0 %all-to-all-start = ((bf16[576,2,128]{2,1,0:T(2,128)(2,1)}), bf16[576,2,128]{2,1,0:T(2,128)(2,1)S(1)}, u32[]{:S(2)}, u32[]{:S(2)}) async-start(bf16[576,2,128]{2,1,0:T(2,128)(2,1)} %bitcast.17), calls=%async_computation | async-start | bytes 589824 | tf_op jit(solution)/shard_map/all_to_all | solution.py:295
  22.8 9.8 %collective-permute-start.3 = (bf16[144,256]{1,0:T(8,128)(2,1)S(1)}, bf16[144,256]{1,0:T(8,128)(2,1)S(1)}, u32[]{:S(2)}, u32[]{:S(2)}) collective-permute-start(bf16[144,256]{1,0:T(8,128)(2,1)S(1)} %shard_map.88), channel_id=1, source_target_pairs={{0,6},{1,7},{2,4},{3,5},{4,2},{5,3},{6,0},{7,1},{8,14},{9,15},{10,... | collective-permute-start | bytes 221192 | tf_op jit(solution)/shard_map/ppermute | solution.py:277
  27.0 7.8 %collective-permute-start.2 = (bf16[144,256]{1,0:T(8,128)(2,1)S(1)}, bf16[144,256]{1,0:T(8,128)(2,1)S(1)}, u32[]{:S(2)}, u32[]{:S(2)}) collective-permute-start(bf16[144,256]{1,0:T(8,128)(2,1)S(1)} %shard_map.88), channel_id=1, source_target_pairs={{0,4},{1,5},{2,6},{3,7},{4,0},{5,1},{6,2},{7,3},{8,12},{9,13},{10,... | collective-permute-start | bytes 221192 | tf_op jit(solution)/shard_map/ppermute | solution.py:277
  29.6 6.5 %collective-permute-start.1 = (bf16[144,256]{1,0:T(8,128)(2,1)S(1)}, bf16[144,256]{1,0:T(8,128)(2,1)S(1)}, u32[]{:S(2)}, u32[]{:S(2)}) collective-permute-start(bf16[144,256]{1,0:T(8,128)(2,1)S(1)} %shard_map.88), channel_id=1, source_target_pairs={{0,2},{1,3},{2,0},{3,1},{4,6},{5,7},{6,4},{7,5},{8,10},{9,11},{10,... | collective-permute-start | bytes 221192 | tf_op jit(solution)/shard_map/ppermute | solution.py:277
  36.1 10.0 %collective-permute-start.4 = (bf16[4,144,256]{2,1,0:T(8,128)(2,1)S(1)}, bf16[4,144,256]{2,1,0:T(8,128)(2,1)S(1)}, u32[]{:S(2)}, u32[]{:S(2)}) collective-permute-start(bf16[4,144,256]{2,1,0:T(8,128)(2,1)S(1)} %pad_maximum_fusion.mine_ref), channel_id=1, source_target_pairs={{0,1},{1,0},{2,3},{3,2},{4,5},{5,4},{6,7},{7,6},{8,9},{9,8},{10,11... | collective-permute-start | bytes 884744 | tf_op jit(solution)/shard_map/ppermute | solution.py:277
  45.0 1.0 %copy-start = (s32[4,3]{1,0:T(4,128)S(1)}, s32[4,3]{1,0:T(4,128)}, u32[]{:S(2)}) copy-start(s32[4,3]{1,0:T(4,128)} %list_ref.1) | copy-start | bytes 148
  47.7 8.3 %collective-permute-start.5 = (bf16[272,128]{1,0:T(8,128)(2,1)S(1)}, bf16[272,128]{1,0:T(8,128)(2,1)S(1)}, u32[]{:S(2)}, u32[]{:S(2)}) collective-permute-start(bf16[272,128]{1,0:T(8,128)(2,1)S(1)} %get-tuple-element.12), channel_id=1, source_target_pairs={{8,16},{24,32},{40,48},{56,64},{72,80},{88,96},{104,112},{120,128}... | collective-permute-start | bytes 208904 | tf_op jit(solution)/shard_map/ppermute | solution.py:273
  53.6 6.2 %collective-permute-start.6 = (bf16[272,128]{1,0:T(8,128)(2,1)S(1)}, bf16[272,128]{1,0:T(8,128)(2,1)S(1)}, u32[]{:S(2)}, u32[]{:S(2)}) collective-permute-start(bf16[272,128]{1,0:T(8,128)(2,1)S(1)} %get-tuple-element.13), channel_id=1, source_target_pairs={{0,8},{16,24},{32,40},{48,56},{64,72},{80,88},{96,104},{112,120},{... | collective-permute-start | bytes 208904 | tf_op jit(solution)/shard_map/ppermute | solution.py:273

commit v4 on v3

--- a/solution.py
+++ b/solution.py
@@ -45,7 +45,28 @@
     return jnp.where(mask, F32(1), F32(0))
 
 
-def prep_kernel(rows_ref, dest_ref, pos_ref, along_ref, across_ref, out_ref):
+def prep_kernel(rows_ref, dest_ref, pos_ref, along_ref, across_ref, out_ref, stage_ref, sems):
+    owner = iota((OWNERS, ROWS), 0)
+    d0, d1 = dest_ref[0:1, :], dest_ref[1:2, :]
+    on0, on1 = ones_where(owner == d0), ones_where(owner == d1)
+    b0, b1 = on0.astype(BF16), on1.astype(BF16)
+    earlier = ones_where(iota((ROWS, ROWS), 0) < iota((ROWS, ROWS), 1)).astype(BF16)
+    rank0 = jnp.sum(on0 * dot(b0, earlier), axis=0, keepdims=True).astype(I32)
+    before1 = dot(b1, earlier) + dot(b0, jnp.ones((ROWS, ROWS), BF16))
+    rank1 = jnp.sum(on1 * before1, axis=0, keepdims=True).astype(I32)
+
+    slot = iota((CAP, ROWS), 0)
+    spreads = []
+    for t, rank in enumerate((rank0, rank1)):
+        position = pos_ref[t : t + 1, :]
+        along = along_ref[t].astype(F32)
+        fields = [(position >> 4).astype(F32), (position & 15).astype(F32)]
+        fields += [along[k : k + 1, :] for k in range(KA)]
+        spread = [jnp.where(slot == rank, field, F32(0)) for field in fields]
+        spread.append(jnp.zeros((HALF - FIELDS * CAP, ROWS), F32))
+        spreads.append(jnp.concatenate(spread, axis=0))
+    spreads = jnp.concatenate(spreads, axis=1).astype(BF16)
+
     taps = across_ref[...].astype(F32)
     products = []
     for half in range(2):
@@ -61,37 +82,25 @@
         products.append(dot(rows_ref[:, first : first + 512], matrix).astype(BF16))
     products = jnp.concatenate(products, axis=0)
 
-    owner = iota((OWNERS, ROWS), 0)
-    d0, d1 = dest_ref[0:1, :], dest_ref[1:2, :]
-    on0, on1 = ones_where(owner == d0), ones_where(owner == d1)
-    b0, b1 = on0.astype(BF16), on1.astype(BF16)
-    earlier = ones_where(iota((ROWS, ROWS), 0) < iota((ROWS, ROWS), 1)).astype(BF16)
-    rank0 = jnp.sum(on0 * dot(b0, earlier), axis=0, keepdims=True).astype(I32)
-    before1 = dot(b1, earlier) + dot(b0, jnp.ones((ROWS, ROWS), BF16))
-    rank1 = jnp.sum(on1 * before1, axis=0, keepdims=True).astype(I32)
-
-    slot = iota((CAP, ROWS), 0)
-    meta = jnp.zeros((OWNERS, HALF), F32)
-    for t, (on, rank) in enumerate(((b0, rank0), (b1, rank1))):
-        position = pos_ref[t : t + 1, :]
-        along = along_ref[t].astype(F32)
-        fields = [(position >> 4).astype(F32), (position & 15).astype(F32)]
-        fields += [along[k : k + 1, :] for k in range(KA)]
-        spread = [jnp.where(slot == rank, field, F32(0)) for field in fields]
-        spread.append(jnp.zeros((HALF - FIELDS * CAP, ROWS), F32))
-        meta = meta + dot_t(on, jnp.concatenate(spread, axis=0).astype(BF16))
-    meta = meta.astype(BF16)
-
     base0, base1 = d0 * CHUNK + 2 * rank0, d1 * CHUNK + 2 * rank1
+    meta0, meta1 = d0 * CHUNK + 2 * CAP, d1 * CHUNK + 2 * CAP
     row = iota((GROUP, ROWS), 0)
-    row_o, col_o = iota((GROUP, OWNERS), 0), iota((GROUP, OWNERS), 1)
+    copies = []
     for g in range(OWNERS // 8):
         n0, n1 = base0 - g * GROUP, base1 - g * GROUP
         left = ones_where((row == n0) | (row == n1))
         right = ones_where((row == n0 + 1) | (row == n1 + 1))
         pick = jnp.concatenate([left, right], axis=1).astype(BF16)
-        place = ones_where(row_o + g * GROUP == col_o * CHUNK + 2 * CAP).astype(BF16)
-        out_ref[g * GROUP : (g + 1) * GROUP, :] = (dot(pick, products) + dot(place, meta)).astype(BF16)
+        place = [ones_where(row == meta - g * GROUP) for meta in (meta0, meta1)]
+        place = jnp.concatenate(place, axis=1).astype(BF16)
+        rows = slice(g * GROUP, (g + 1) * GROUP)
+        stage_ref[rows, :] = (dot(pick, products) + dot_t(place, spreads)).astype(BF16)
+        if g % 4 == 3:
+            rows = slice((g - 3) * GROUP, (g + 1) * GROUP)
+            copies.append(pltpu.make_async_copy(stage_ref.at[rows], out_ref.at[rows], sems.at[g // 4]))
+            copies[-1].start()
+    for copy in copies:
+        copy.wait()
 
 
 def shade_of(z, up, down):
@@ -169,8 +178,6 @@
     border_ref,
     reduced_ref,
     column_ref,
-    stage_ref,
-    sems,
 ):
     tile_me = lax.axis_index("tile")
     band_me = lax.axis_index("bands")
@@ -192,7 +199,6 @@
     last_shade = shade_of(last, before_last, jnp.where(row == 7, edge[0:1], pltpu.roll(first, 7, 0)))
 
     cols_of = ones_where((iota((TILE, HALF), 0) >> 1) == iota((TILE, HALF), 1)).astype(BF16)
-    copies = []
     for tile in range(TILES):
         shade = []
         for i, block in enumerate(two_blocks(tile, slice(0, ROWS))):
@@ -202,12 +208,10 @@
             shade.append(jnp.where(row == 7, last_shade[b : b + 1], block[-8:]))
         rows = slice(tile * TILE, (tile + 1) * TILE)
         finished = (resampled_ref[rows, :] * jnp.concatenate(shade, axis=0)).astype(BF16)
-        stage_ref[rows, :] = finished
-        copy = pltpu.make_async_copy(stage_ref.at[rows], out_ref.at[rows], sems.at[tile])
-        copy.start()
-        copies.append(copy)
-        column_ref[...] = dot(finished, cols_of)
-        reduced_ref[tile] = (column_ref[pl.ds(0, HALF, stride=2), :] + column_ref[pl.ds(1, HALF, stride=2), :]) * 0.25
+        out_ref[rows, :] = finished
+        column_ref[rows, :] = dot(finished, cols_of)
+        even, odd = [column_ref[pl.ds(tile * TILE + i, HALF, stride=2), :] for i in range(2)]
+        reduced_ref[tile] = (even + odd) * 0.25
 
     part_ref[...] = jnp.zeros(part_ref.shape, F32)
     near_ref[...] = jnp.zeros(near_ref.shape, BF16)
@@ -237,23 +241,34 @@
     eighth = iota((16, HALF), 0) < 8
     for way, ref in enumerate((near_ref, far_ref)):
         ref[2 * HALF :, :] = jnp.where(eighth, codes[way][0], codes[way][1]).astype(F32).astype(BF16)
-    for copy in copies:
-        copy.wait()
-
-
-def combine_kernel(part_ref, far_ref, near_ref, out_ref):
+
+
+def store_kernel(finished_ref, out_ref, sem):
+    copy = pltpu.make_async_copy(finished_ref, out_ref, sem)
+    copy.start()
+    copy.wait()
+
+
+def combine_kernel(part_ref, far_ref, near_ref, out_ref, stage_ref, sems):
     arrived = []
     for ref in (far_ref, near_ref):
         codes = ref[2 * HALF :, :].astype(F32)
         for s in range(2):
             arrived.append((codes[8 * s : 8 * s + 1], ref[s * HALF : (s + 1) * HALF, :].astype(F32)))
-    for place in range(8):
-        total = part_ref[place]
-        for code, tile in arrived:
-            total = total + jnp.where(code == F32(place + 1), tile, F32(0))
-        level, quadrant = divmod(place, 4)
-        top, left = quadrant // 2 * HALF, quadrant % 2 * HALF
-        out_ref[level, top : top + HALF, left : left + HALF] = total.astype(BF16)
+    copies = []
+    for level in range(2):
+        for quadrant in range(4):
+            place = 4 * level + quadrant
+            total = part_ref[place]
+            for code, tile in arrived:
+                total = total + jnp.where(code == F32(place + 1), tile, F32(0))
+            top, left = quadrant // 2 * HALF, quadrant % 2 * HALF
+            stage_ref[level, top : top + HALF, left : left + HALF] = total.astype(BF16)
+        copy = pltpu.make_async_copy(stage_ref.at[level], out_ref.at[level], sems.at[level])
+        copy.start()
+        copies.append(copy)
+    for copy in copies:
+        copy.wait()
 
 
 def call(kernel, outs, ins, scratch=(), cost=None, params=PARAMS, out_specs=None):
@@ -279,7 +294,14 @@
 
 def shards(scene_rows, row_dest, row_pos, along_taps, across_taps, elevation, pyramid_list):
     shape = jax.ShapeDtypeStruct
-    outgoing = call(prep_kernel, shape((OWNERS * CHUNK, HALF), BF16), [VMEM] * 5, params=pltpu.CompilerParams(vmem_limit_bytes=60 * 1024 * 1024))(
+    outgoing = call(
+        prep_kernel,
+        shape((OWNERS * CHUNK, HALF), BF16),
+        [VMEM] * 5,
+        [pltpu.VMEM((OWNERS * CHUNK, HALF), BF16), pltpu.SemaphoreType.DMA((2,))],
+        params=pltpu.CompilerParams(vmem_limit_bytes=60 * 1024 * 1024),
+        out_specs=pl.BlockSpec(memory_space=pl.ANY),
+    )(
         scene_rows[0],
         row_dest.T,
         row_pos.T,
@@ -317,14 +339,25 @@
         [
             pltpu.VMEM((5, 8, TILE), F32),
             pltpu.VMEM((TILES, HALF, HALF), F32),
-            pltpu.VMEM((TILE, HALF), F32),
-            pltpu.VMEM((TILES * TILE, TILE), BF16),
-            pltpu.SemaphoreType.DMA((TILES,)),
+            pltpu.VMEM((TILES * TILE, HALF), F32),
         ],
-        out_specs=(pl.BlockSpec(memory_space=pl.ANY), VMEM, VMEM, VMEM),
     )(resampled, mine, theirs, pyramid_list)
     far, near = swap(far, 1), swap(near, 0)
-    pyramid = call(combine_kernel, shape((2, TILE, TILE), BF16), [VMEM] * 3)(part, far, near)
+    finished = call(
+        store_kernel,
+        shape((TILES * TILE, TILE), BF16),
+        [VMEM],
+        [pltpu.SemaphoreType.DMA],
+        pl.CostEstimate(flops=0, bytes_accessed=1_000_000, transcendentals=0),
+        out_specs=pl.BlockSpec(memory_space=pl.ANY),
+    )(finished)
+    pyramid = call(
+        combine_kernel,
+        shape((2, TILE, TILE), BF16),
+        [VMEM] * 3,
+        [pltpu.VMEM((2, TILE, TILE), BF16), pltpu.SemaphoreType.DMA((2,))],
+        out_specs=pl.BlockSpec(memory_space=pl.ANY),
+    )(part, far, near)
     return (finished[None], pyramid[None])
 
 

time: 61.1 us -> 60.4 us (0.989)
  waiting for transfers between devices: 14.7 us -> 13.8 us
    ppermute x2, waiting for transfers between devices: 4.27 us -> 3.46 us  [swap(): return lax.ppermute(value, 'tile', pairs + [(j, i) for i, j in pairs])]
    pallas_call x2 -> x3, Pallas kernels: 3.64 us -> 4.21 us  [the longest x1 2.55 us: shards(): call(prep_kernel, shape((OWNERS * CHUNK, HALF), BF16), [VMEM] * 5, [pltpu...]
  transfers between devices with their start and end apart: 8 -> 8, of which waited for: 5 -> 4; matrix products, arithmetic and copies ran while one was open for 0% -> 0% of each run, Pallas kernels for 7% -> 8%
where the time goes in v4:
time: 60.4 us; the launch traced here: 60.1 us
  starting transfers between devices  38.8 us (64%)
  waiting for transfers between devices  13.8 us (23%)
  Pallas kernels  6.59 us (11%)
  between operations  0.79 us (1%)
    all_to_all x1, starting transfers between devices, shards(): lax.all_to_all(units, 'tile', split_axis=0, concat_axis=0, tiled=True)  18.5 us
    ppermute x4, starting transfers between devices, exchange(): lax.ppermute(value, 'bands', [(i, i ^ mask) for i in range(lax.axis_size(...  11.7 us
    ppermute x2, starting transfers between devices, swap(): return lax.ppermute(value, 'tile', pairs + [(j, i) for i, j in pairs])  7.85 us
    all_to_all x1, waiting for transfers between devices, shards(): lax.all_to_all(units, 'tile', split_axis=0, concat_axis=0, tiled=True)  7.01 us
    ppermute x2, waiting for transfers between devices, swap(): return lax.ppermute(value, 'tile', pairs + [(j, i) for i, j in pairs])  3.46 us
    ppermute x4, waiting for transfers between devices, exchange(): lax.ppermute(value, 'bands', [(i, i ^ mask) for i in range(lax.axis_size(...  3.37 us
    pallas_call x1, Pallas kernels, shards(): call(prep_kernel, shape((OWNERS * CHUNK, HALF), BF16), [VMEM] * 5, [pltpu...  2.55 us
  transfers between devices with their start and end apart: 8, of which 4 were waited for; matrix products, arithmetic and copies ran while one was open for 0% of the time, Pallas kernels for 8%

profile of v4, /device:TPU:38, one launch (start us, length us, event | category | flops | bytes accessed | tf_op | source)
XLA Modules:
  0.0 60.1 jit_solution(9325760364504189476)
XLA Ops:
  0.6 0.7 %collective-permute-start = (f32[128,256]{1,0:T(8,128)}, f32[128,256]{1,0:T(8,128)S(1)}, u32[]{:S(2)}, u32[]{:S(2)}) collective-permute-start(f32[128,256]{1,0:T(8,128)} %z_ref), channel_id=1, source_target_pairs={{8,0},{16,8},{24,16},{32,24},{40,32},{48,40},{56,48},{64,56},{72,6... | collective-permute-start | bytes 393224 | tf_op jit(solution)/shard_map/ppermute | solution.py:314
  1.3 2.6 %shard_map.86 = bf16[1152,128]{1,0:T(8,128)(2,1)} custom-call(bf16[128,768]{1,0:T(8,128)(2,1)} %bitcast.20, s32[2,128]{1,0:T(2,128)} %bitcast.26, s32[2,128]{1,0:T(2,128)} %bitcast.27, bf16[2,4,128]{2,1,0:T(4,128)(2,1)} %bitcast.25, bf16[8,256]{1,0:T(8,128)(2,1)} %bitcast.24), custom_call_target="tpu_custom_call" | custom-call | tf_op jit(solution)/shard_map/pallas_call | solution.py:297
  3.9 0.0 copy-start.1
  3.9 18.5 %all-to-all-start = ((bf16[576,2,128]{2,1,0:T(2,128)(2,1)}), bf16[576,2,128]{2,1,0:T(2,128)(2,1)S(1)}, u32[]{:S(2)}, u32[]{:S(2)}) async-start(bf16[576,2,128]{2,1,0:T(2,128)(2,1)} %bitcast.17), calls=%async_computation | async-start | bytes 589824 | tf_op jit(solution)/shard_map/all_to_all | solution.py:317
  22.4 0.0 collective-permute-done.beside_ref
  22.4 0.0 copy-done.1
  22.4 0.2 shard_map.88
  22.6 4.2 %collective-permute-start.3 = (bf16[144,256]{1,0:T(8,128)(2,1)S(1)}, bf16[144,256]{1,0:T(8,128)(2,1)S(1)}, u32[]{:S(2)}, u32[]{:S(2)}) collective-permute-start(bf16[144,256]{1,0:T(8,128)(2,1)S(1)} %shard_map.88), channel_id=1, source_target_pairs={{0,6},{1,7},{2,4},{3,5},{4,2},{5,3},{6,0},{7,1},{8,14},{9,15},{10,... | collective-permute-start | bytes 221192 | tf_op jit(solution)/shard_map/ppermute | solution.py:292
  26.8 2.5 %collective-permute-start.2 = (bf16[144,256]{1,0:T(8,128)(2,1)S(1)}, bf16[144,256]{1,0:T(8,128)(2,1)S(1)}, u32[]{:S(2)}, u32[]{:S(2)}) collective-permute-start(bf16[144,256]{1,0:T(8,128)(2,1)S(1)} %shard_map.88), channel_id=1, source_target_pairs={{0,4},{1,5},{2,6},{3,7},{4,0},{5,1},{6,2},{7,3},{8,12},{9,13},{10,... | collective-permute-start | bytes 221192 | tf_op jit(solution)/shard_map/ppermute | solution.py:292
  29.4 3.1 %collective-permute-start.1 = (bf16[144,256]{1,0:T(8,128)(2,1)S(1)}, bf16[144,256]{1,0:T(8,128)(2,1)S(1)}, u32[]{:S(2)}, u32[]{:S(2)}) collective-permute-start(bf16[144,256]{1,0:T(8,128)(2,1)S(1)} %shard_map.88), channel_id=1, source_target_pairs={{0,2},{1,3},{2,0},{3,1},{4,6},{5,7},{6,4},{7,5},{8,10},{9,11},{10,... | collective-permute-start | bytes 221192 | tf_op jit(solution)/shard_map/ppermute | solution.py:292
  32.5 0.0 collective-permute-done.3
  32.5 2.1 %collective-permute-done.2 = bf16[144,256]{1,0:T(8,128)(2,1)S(1)} collective-permute-done((bf16[144,256]{1,0:T(8,128)(2,1)S(1)}, bf16[144,256]{1,0:T(8,128)(2,1)S(1)}, u32[]{:S(2)}, u32[]{:S(2)}) %collective-permute-start.2) | collective-permute-done | bytes 73760 | tf_op jit(solution)/shard_map/ppermute | solution.py:292
  34.6 1.3 %collective-permute-done.1 = bf16[144,256]{1,0:T(8,128)(2,1)S(1)} collective-permute-done((bf16[144,256]{1,0:T(8,128)(2,1)S(1)}, bf16[144,256]{1,0:T(8,128)(2,1)S(1)}, u32[]{:S(2)}, u32[]{:S(2)}) %collective-permute-start.1) | collective-permute-done | bytes 73760 | tf_op jit(solution)/shard_map/ppermute | solution.py:292
  35.9 1.9 %collective-permute-start.4 = (bf16[4,144,256]{2,1,0:T(8,128)(2,1)S(1)}, bf16[4,144,256]{2,1,0:T(8,128)(2,1)S(1)}, u32[]{:S(2)}, u32[]{:S(2)}) collective-permute-start(bf16[4,144,256]{2,1,0:T(8,128)(2,1)S(1)} %pad_maximum_fusion.mine_ref), channel_id=1, source_target_pairs={{0,1},{1,0},{2,3},{3,2},{4,5},{5,4},{6,7},{7,6},{8,9},{9,8},{10,11... | collective-permute-start | bytes 884744 | tf_op jit(solution)/shard_map/ppermute | solution.py:292
  37.8 7.0 %all-to-all-done = bf16[576,2,128]{2,1,0:T(2,128)(2,1)S(1)} async-done(((bf16[576,2,128]{2,1,0:T(2,128)(2,1)}), bf16[576,2,128]{2,1,0:T(2,128)(2,1)S(1)}, u32[]{:S(2)}, u32[]{:S(2)}) %all-to-all-start) | async-done | bytes 294944 | tf_op jit(solution)/shard_map/all_to_all | solution.py:317
  44.8 0.0 copy-start
  44.8 1.0 %shard_map.87.resampled_ref = f32[1024,256]{1,0:T(8,128)S(1)} custom-call(bf16[1152,128]{1,0:T(8,128)(2,1)S(1)} %bitcast.15), custom_call_target="tpu_custom_call" | custom-call | flops 400000000 | bytes 1500000 | tf_op jit(solution)/shard_map/pallas_call | solution.py:323
  45.9 0.0 collective-permute-done.4.theirs_ref
  45.9 0.0 copy-done
  45.9 1.2 %shard_map.89 = (bf16[1024,256]{1,0:T(8,128)(2,1)S(1)}, f32[8,128,128]{2,1,0:T(8,128)S(1)}, bf16[272,128]{1,0:T(8,128)(2,1)S(1)}, bf16[272,128]{1,0:T(8,128)(2,1)S(1)}) custom-call(f32[1024,256]{1,0:T(8,128)S(1)} %shard_map.87.resampled_ref, bf16[4,144,256]{2,1,0:T(8,128)(2,1)S(1)} %pad_maximum_fusion.mine_ref, ...), custom_call_target="tpu_custom_call" | custom-call | tf_op jit(solution)/shard_map/pallas_call | solution.py:330
  47.1 5.9 %collective-permute-start.5 = (bf16[272,128]{1,0:T(8,128)(2,1)S(1)}, bf16[272,128]{1,0:T(8,128)(2,1)S(1)}, u32[]{:S(2)}, u32[]{:S(2)}) collective-permute-start(bf16[272,128]{1,0:T(8,128)(2,1)S(1)} %get-tuple-element.12), channel_id=1, source_target_pairs={{8,16},{24,32},{40,48},{56,64},{72,80},{88,96},{104,112},{120,128}... | collective-permute-start | bytes 208904 | tf_op jit(solution)/shard_map/ppermute | solution.py:288
  53.0 1.9 %collective-permute-start.6 = (bf16[272,128]{1,0:T(8,128)(2,1)S(1)}, bf16[272,128]{1,0:T(8,128)(2,1)S(1)}, u32[]{:S(2)}, u32[]{:S(2)}) collective-permute-start(bf16[272,128]{1,0:T(8,128)(2,1)S(1)} %get-tuple-element.13), channel_id=1, source_target_pairs={{0,8},{16,24},{32,40},{48,56},{64,72},{80,88},{96,104},{112,120},{... | collective-permute-start | bytes 208904 | tf_op jit(solution)/shard_map/ppermute | solution.py:288
  54.9 0.8 %shard_map.90 = bf16[1024,256]{1,0:T(8,128)(2,1)} custom-call(bf16[1024,256]{1,0:T(8,128)(2,1)S(1)} %get-tuple-element.10.finished_ref), custom_call_target="tpu_custom_call" | custom-call | bytes 1000000 | tf_op jit(solution)/shard_map/pallas_call | solution.py:346
  55.7 0.0 collective-permute-done.5.far_ref
  55.7 3.5 %collective-permute-done.6.near_ref = bf16[272,128]{1,0:T(8,128)(2,1)S(1)} collective-permute-done((bf16[272,128]{1,0:T(8,128)(2,1)S(1)}, bf16[272,128]{1,0:T(8,128)(2,1)S(1)}, u32[]{:S(2)}, u32[]{:S(2)}) %collective-permute-start.6) | collective-permute-done | bytes 69664 | tf_op jit(solution)/shard_map/ppermute | solution.py:288
  59.2 0.9 %shard_map.91 = bf16[2,256,256]{2,1,0:T(8,128)(2,1)} custom-call(f32[8,128,128]{2,1,0:T(8,128)S(1)} %get-tuple-element.11.part_ref, bf16[272,128]{1,0:T(8,128)(2,1)S(1)} %collective-permute-done.5.far_ref, bf16[272,128]{1,0:T(8,128)(2,1)S(1)} %collective-permute-done.6.near_ref), custom_call_target="tpu_custom_call" | custom-call | tf_op jit(solution)/shard_map/pallas_call | solution.py:354
  (1 shorter events, 0.0 us)
Async XLA Ops:
  0.6 21.8 %collective-permute-start = (f32[128,256]{1,0:T(8,128)}, f32[128,256]{1,0:T(8,128)S(1)}, u32[]{:S(2)}, u32[]{:S(2)}) collective-permute-start(f32[128,256]{1,0:T(8,128)} %z_ref), channel_id=1, source_target_pairs={{8,0},{16,8},{24,16},{32,24},{40,32},{48,40},{56,48},{64,56},{72,6... | collective-permute-start | bytes 393224 | tf_op jit(solution)/shard_map/ppermute | solution.py:314
  3.9 18.6 %copy-start.1 = (f32[128,256]{1,0:T(8,128)S(1)}, f32[128,256]{1,0:T(8,128)}, u32[]{:S(2)}) copy-start(f32[128,256]{1,0:T(8,128)} %z_ref) | copy-start | bytes 393220
  3.9 41.0 %all-to-all-start = ((bf16[576,2,128]{2,1,0:T(2,128)(2,1)}), bf16[576,2,128]{2,1,0:T(2,128)(2,1)S(1)}, u32[]{:S(2)}, u32[]{:S(2)}) async-start(bf16[576,2,128]{2,1,0:T(2,128)(2,1)} %bitcast.17), calls=%async_computation | async-start | bytes 589824 | tf_op jit(solution)/shard_map/all_to_all | solution.py:317
  22.6 9.8 %collective-permute-start.3 = (bf16[144,256]{1,0:T(8,128)(2,1)S(1)}, bf16[144,256]{1,0:T(8,128)(2,1)S(1)}, u32[]{:S(2)}, u32[]{:S(2)}) collective-permute-start(bf16[144,256]{1,0:T(8,128)(2,1)S(1)} %shard_map.88), channel_id=1, source_target_pairs={{0,6},{1,7},{2,4},{3,5},{4,2},{5,3},{6,0},{7,1},{8,14},{9,15},{10,... | collective-permute-start | bytes 221192 | tf_op jit(solution)/shard_map/ppermute | solution.py:292
  26.8 7.8 %collective-permute-start.2 = (bf16[144,256]{1,0:T(8,128)(2,1)S(1)}, bf16[144,256]{1,0:T(8,128)(2,1)S(1)}, u32[]{:S(2)}, u32[]{:S(2)}) collective-permute-start(bf16[144,256]{1,0:T(8,128)(2,1)S(1)} %shard_map.88), channel_id=1, source_target_pairs={{0,4},{1,5},{2,6},{3,7},{4,0},{5,1},{6,2},{7,3},{8,12},{9,13},{10,... | collective-permute-start | bytes 221192 | tf_op jit(solution)/shard_map/ppermute | solution.py:292
  29.4 6.5 %collective-permute-start.1 = (bf16[144,256]{1,0:T(8,128)(2,1)S(1)}, bf16[144,256]{1,0:T(8,128)(2,1)S(1)}, u32[]{:S(2)}, u32[]{:S(2)}) collective-permute-start(bf16[144,256]{1,0:T(8,128)(2,1)S(1)} %shard_map.88), channel_id=1, source_target_pairs={{0,2},{1,3},{2,0},{3,1},{4,6},{5,7},{6,4},{7,5},{8,10},{9,11},{10,... | collective-permute-start | bytes 221192 | tf_op jit(solution)/shard_map/ppermute | solution.py:292
  35.9 10.0 %collective-permute-start.4 = (bf16[4,144,256]{2,1,0:T(8,128)(2,1)S(1)}, bf16[4,144,256]{2,1,0:T(8,128)(2,1)S(1)}, u32[]{:S(2)}, u32[]{:S(2)}) collective-permute-start(bf16[4,144,256]{2,1,0:T(8,128)(2,1)S(1)} %pad_maximum_fusion.mine_ref), channel_id=1, source_target_pairs={{0,1},{1,0},{2,3},{3,2},{4,5},{5,4},{6,7},{7,6},{8,9},{9,8},{10,11... | collective-permute-start | bytes 884744 | tf_op jit(solution)/shard_map/ppermute | solution.py:292
  44.8 1.0 %copy-start = (s32[4,3]{1,0:T(4,128)S(1)}, s32[4,3]{1,0:T(4,128)}, u32[]{:S(2)}) copy-start(s32[4,3]{1,0:T(4,128)} %list_ref.1) | copy-start | bytes 148
  47.1 8.7 %collective-permute-start.5 = (bf16[272,128]{1,0:T(8,128)(2,1)S(1)}, bf16[272,128]{1,0:T(8,128)(2,1)S(1)}, u32[]{:S(2)}, u32[]{:S(2)}) collective-permute-start(bf16[272,128]{1,0:T(8,128)(2,1)S(1)} %get-tuple-element.12), channel_id=1, source_target_pairs={{8,16},{24,32},{40,48},{56,64},{72,80},{88,96},{104,112},{120,128}... | collective-permute-start | bytes 208904 | tf_op jit(solution)/shard_map/ppermute | solution.py:288
  53.0 6.2 %collective-permute-start.6 = (bf16[272,128]{1,0:T(8,128)(2,1)S(1)}, bf16[272,128]{1,0:T(8,128)(2,1)S(1)}, u32[]{:S(2)}, u32[]{:S(2)}) collective-permute-start(bf16[272,128]{1,0:T(8,128)(2,1)S(1)} %get-tuple-element.13), channel_id=1, source_target_pairs={{0,8},{16,24},{32,40},{48,56},{64,72},{80,88},{96,104},{112,120},{... | collective-permute-start | bytes 208904 | tf_op jit(solution)/shard_map/ppermute | solution.py:288

commit v5 on v4

--- a/solution.py
+++ b/solution.py
@@ -124,19 +124,17 @@
 
 
 def resample_kernel(recv_ref, out_ref, across_ref, meta_ref):
-    row, col = iota((GROUP, GROUP), 0), iota((GROUP, GROUP), 1)
+    row, col = iota((16, GROUP), 0), iota((16, GROUP), 1)
+    pick = ones_where(col == CHUNK * row + 2 * CAP).astype(BF16)
+    for g in range(OWNERS // 8):
+        meta_ref[g * 8 : (g + 1) * 8, :] = dot(pick, recv_ref[g * GROUP : (g + 1) * GROUP, :])[:8]
+    row, col = iota((2 * 64, GROUP), 0), iota((2 * 64, GROUP), 1)
     slot = row & 63
-    target = jnp.where(
-        row < 2 * 64,
-        CHUNK * (slot >> 3) + 2 * (slot & 7) + (row >> 6),
-        jnp.where(row < 2 * 64 + 8, CHUNK * slot + 2 * CAP, -1),
-    )
-    pick = ones_where(col == target).astype(BF16)
+    pick = ones_where(col == CHUNK * (slot >> 3) + 2 * (slot & 7) + (row >> 6)).astype(BF16)
     for g in range(OWNERS // 8):
         parts = dot(pick, recv_ref[g * GROUP : (g + 1) * GROUP, :])
         across_ref[g * 64 : (g + 1) * 64, :HALF] = parts[:64].astype(BF16)
-        across_ref[g * 64 : (g + 1) * 64, HALF:] = parts[64:128].astype(BF16)
-        meta_ref[g * 8 : (g + 1) * 8, :] = parts[128:136]
+        across_ref[g * 64 : (g + 1) * 64, HALF:] = parts[64:].astype(BF16)
     slots = OWNERS * CAP
     meta = meta_ref[...]
     rolled = [meta] + [pltpu.roll(meta, HALF - CAP * f, 1) for f in range(1, FIELDS)]

time: 60.4 us -> 60.3 us (level)
  transfers between devices with their start and end apart: 8 -> 8, of which waited for: 4 -> 4; matrix products, arithmetic and copies ran while one was open for 0% -> 0% of each run, Pallas kernels for 8% -> 7%
where the time goes in v5:
time: 60.3 us; the launch traced here: 60 us
  starting transfers between devices  38.8 us (64%)
  waiting for transfers between devices  13.8 us (23%)
  Pallas kernels  6.51 us (11%)
  between operations  0.79 us (1%)
    all_to_all x1, starting transfers between devices, shards(): lax.all_to_all(units, 'tile', split_axis=0, concat_axis=0, tiled=True)  18.5 us
    ppermute x4, starting transfers between devices, exchange(): lax.ppermute(value, 'bands', [(i, i ^ mask) for i in range(lax.axis_size(...  11.7 us
    ppermute x2, starting transfers between devices, swap(): return lax.ppermute(value, 'tile', pairs + [(j, i) for i, j in pairs])  7.85 us
    all_to_all x1, waiting for transfers between devices, shards(): lax.all_to_all(units, 'tile', split_axis=0, concat_axis=0, tiled=True)  7.01 us
    ppermute x2, waiting for transfers between devices, swap(): return lax.ppermute(value, 'tile', pairs + [(j, i) for i, j in pairs])  3.46 us
    ppermute x4, waiting for transfers between devices, exchange(): lax.ppermute(value, 'bands', [(i, i ^ mask) for i in range(lax.axis_size(...  3.37 us
    pallas_call x1, Pallas kernels, shards(): call(prep_kernel, shape((OWNERS * CHUNK, HALF), BF16), [VMEM] * 5, [pltpu...  2.55 us
  transfers between devices with their start and end apart: 8, of which 4 were waited for; matrix products, arithmetic and copies ran while one was open for 0% of the time, Pallas kernels for 7%

profile of v5, /device:TPU:38, one launch (start us, length us, event | category | flops | bytes accessed | tf_op | source)
XLA Modules:
  0.0 60.0 jit_solution(16607640987306166680)
XLA Ops:
  0.6 0.7 %collective-permute-start = (f32[128,256]{1,0:T(8,128)}, f32[128,256]{1,0:T(8,128)S(1)}, u32[]{:S(2)}, u32[]{:S(2)}) collective-permute-start(f32[128,256]{1,0:T(8,128)} %z_ref), channel_id=1, source_target_pairs={{8,0},{16,8},{24,16},{32,24},{40,32},{48,40},{56,48},{64,56},{72,6... | collective-permute-start | bytes 393224 | tf_op jit(solution)/shard_map/ppermute | solution.py:312
  1.3 2.6 %shard_map.86 = bf16[1152,128]{1,0:T(8,128)(2,1)} custom-call(bf16[128,768]{1,0:T(8,128)(2,1)} %bitcast.20, s32[2,128]{1,0:T(2,128)} %bitcast.26, s32[2,128]{1,0:T(2,128)} %bitcast.27, bf16[2,4,128]{2,1,0:T(4,128)(2,1)} %bitcast.25, bf16[8,256]{1,0:T(8,128)(2,1)} %bitcast.24), custom_call_target="tpu_custom_call" | custom-call | tf_op jit(solution)/shard_map/pallas_call | solution.py:295
  3.9 0.0 copy-start.1
  3.9 18.5 %all-to-all-start = ((bf16[576,2,128]{2,1,0:T(2,128)(2,1)}), bf16[576,2,128]{2,1,0:T(2,128)(2,1)S(1)}, u32[]{:S(2)}, u32[]{:S(2)}) async-start(bf16[576,2,128]{2,1,0:T(2,128)(2,1)} %bitcast.17), calls=%async_computation | async-start | bytes 589824 | tf_op jit(solution)/shard_map/all_to_all | solution.py:315
  22.4 0.0 collective-permute-done.beside_ref
  22.4 0.0 copy-done.1
  22.4 0.2 shard_map.88
  22.6 4.2 %collective-permute-start.3 = (bf16[144,256]{1,0:T(8,128)(2,1)S(1)}, bf16[144,256]{1,0:T(8,128)(2,1)S(1)}, u32[]{:S(2)}, u32[]{:S(2)}) collective-permute-start(bf16[144,256]{1,0:T(8,128)(2,1)S(1)} %shard_map.88), channel_id=1, source_target_pairs={{0,6},{1,7},{2,4},{3,5},{4,2},{5,3},{6,0},{7,1},{8,14},{9,15},{10,... | collective-permute-start | bytes 221192 | tf_op jit(solution)/shard_map/ppermute | solution.py:290
  26.8 2.5 %collective-permute-start.2 = (bf16[144,256]{1,0:T(8,128)(2,1)S(1)}, bf16[144,256]{1,0:T(8,128)(2,1)S(1)}, u32[]{:S(2)}, u32[]{:S(2)}) collective-permute-start(bf16[144,256]{1,0:T(8,128)(2,1)S(1)} %shard_map.88), channel_id=1, source_target_pairs={{0,4},{1,5},{2,6},{3,7},{4,0},{5,1},{6,2},{7,3},{8,12},{9,13},{10,... | collective-permute-start | bytes 221192 | tf_op jit(solution)/shard_map/ppermute | solution.py:290
  29.4 3.1 %collective-permute-start.1 = (bf16[144,256]{1,0:T(8,128)(2,1)S(1)}, bf16[144,256]{1,0:T(8,128)(2,1)S(1)}, u32[]{:S(2)}, u32[]{:S(2)}) collective-permute-start(bf16[144,256]{1,0:T(8,128)(2,1)S(1)} %shard_map.88), channel_id=1, source_target_pairs={{0,2},{1,3},{2,0},{3,1},{4,6},{5,7},{6,4},{7,5},{8,10},{9,11},{10,... | collective-permute-start | bytes 221192 | tf_op jit(solution)/shard_map/ppermute | solution.py:290
  32.5 0.0 collective-permute-done.3
  32.5 2.1 %collective-permute-done.2 = bf16[144,256]{1,0:T(8,128)(2,1)S(1)} collective-permute-done((bf16[144,256]{1,0:T(8,128)(2,1)S(1)}, bf16[144,256]{1,0:T(8,128)(2,1)S(1)}, u32[]{:S(2)}, u32[]{:S(2)}) %collective-permute-start.2) | collective-permute-done | bytes 73760 | tf_op jit(solution)/shard_map/ppermute | solution.py:290
  34.6 1.3 %collective-permute-done.1 = bf16[144,256]{1,0:T(8,128)(2,1)S(1)} collective-permute-done((bf16[144,256]{1,0:T(8,128)(2,1)S(1)}, bf16[144,256]{1,0:T(8,128)(2,1)S(1)}, u32[]{:S(2)}, u32[]{:S(2)}) %collective-permute-start.1) | collective-permute-done | bytes 73760 | tf_op jit(solution)/shard_map/ppermute | solution.py:290
  35.9 1.9 %collective-permute-start.4 = (bf16[4,144,256]{2,1,0:T(8,128)(2,1)S(1)}, bf16[4,144,256]{2,1,0:T(8,128)(2,1)S(1)}, u32[]{:S(2)}, u32[]{:S(2)}) collective-permute-start(bf16[4,144,256]{2,1,0:T(8,128)(2,1)S(1)} %pad_maximum_fusion.mine_ref), channel_id=1, source_target_pairs={{0,1},{1,0},{2,3},{3,2},{4,5},{5,4},{6,7},{7,6},{8,9},{9,8},{10,11... | collective-permute-start | bytes 884744 | tf_op jit(solution)/shard_map/ppermute | solution.py:290
  37.8 7.0 %all-to-all-done = bf16[576,2,128]{2,1,0:T(2,128)(2,1)S(1)} async-done(((bf16[576,2,128]{2,1,0:T(2,128)(2,1)}), bf16[576,2,128]{2,1,0:T(2,128)(2,1)S(1)}, u32[]{:S(2)}, u32[]{:S(2)}) %all-to-all-start) | async-done | bytes 294944 | tf_op jit(solution)/shard_map/all_to_all | solution.py:315
  44.8 0.0 copy-start
  44.8 0.9 %shard_map.87.resampled_ref = f32[1024,256]{1,0:T(8,128)S(1)} custom-call(bf16[1152,128]{1,0:T(8,128)(2,1)S(1)} %bitcast.15), custom_call_target="tpu_custom_call" | custom-call | flops 400000000 | bytes 1500000 | tf_op jit(solution)/shard_map/pallas_call | solution.py:321
  45.8 0.0 collective-permute-done.4.theirs_ref
  45.8 0.0 copy-done
  45.8 1.2 %shard_map.89 = (bf16[1024,256]{1,0:T(8,128)(2,1)S(1)}, f32[8,128,128]{2,1,0:T(8,128)S(1)}, bf16[272,128]{1,0:T(8,128)(2,1)S(1)}, bf16[272,128]{1,0:T(8,128)(2,1)S(1)}) custom-call(f32[1024,256]{1,0:T(8,128)S(1)} %shard_map.87.resampled_ref, bf16[4,144,256]{2,1,0:T(8,128)(2,1)S(1)} %pad_maximum_fusion.mine_ref, ...), custom_call_target="tpu_custom_call" | custom-call | tf_op jit(solution)/shard_map/pallas_call | solution.py:328
  47.0 5.9 %collective-permute-start.5 = (bf16[272,128]{1,0:T(8,128)(2,1)S(1)}, bf16[272,128]{1,0:T(8,128)(2,1)S(1)}, u32[]{:S(2)}, u32[]{:S(2)}) collective-permute-start(bf16[272,128]{1,0:T(8,128)(2,1)S(1)} %get-tuple-element.12), channel_id=1, source_target_pairs={{8,16},{24,32},{40,48},{56,64},{72,80},{88,96},{104,112},{120,128}... | collective-permute-start | bytes 208904 | tf_op jit(solution)/shard_map/ppermute | solution.py:286
  52.9 1.9 %collective-permute-start.6 = (bf16[272,128]{1,0:T(8,128)(2,1)S(1)}, bf16[272,128]{1,0:T(8,128)(2,1)S(1)}, u32[]{:S(2)}, u32[]{:S(2)}) collective-permute-start(bf16[272,128]{1,0:T(8,128)(2,1)S(1)} %get-tuple-element.13), channel_id=1, source_target_pairs={{0,8},{16,24},{32,40},{48,56},{64,72},{80,88},{96,104},{112,120},{... | collective-permute-start | bytes 208904 | tf_op jit(solution)/shard_map/ppermute | solution.py:286
  54.8 0.8 %shard_map.90 = bf16[1024,256]{1,0:T(8,128)(2,1)} custom-call(bf16[1024,256]{1,0:T(8,128)(2,1)S(1)} %get-tuple-element.10.finished_ref), custom_call_target="tpu_custom_call" | custom-call | bytes 1000000 | tf_op jit(solution)/shard_map/pallas_call | solution.py:344
  55.6 0.0 collective-permute-done.5.far_ref
  55.7 3.5 %collective-permute-done.6.near_ref = bf16[272,128]{1,0:T(8,128)(2,1)S(1)} collective-permute-done((bf16[272,128]{1,0:T(8,128)(2,1)S(1)}, bf16[272,128]{1,0:T(8,128)(2,1)S(1)}, u32[]{:S(2)}, u32[]{:S(2)}) %collective-permute-start.6) | collective-permute-done | bytes 69664 | tf_op jit(solution)/shard_map/ppermute | solution.py:286
  59.1 0.9 %shard_map.91 = bf16[2,256,256]{2,1,0:T(8,128)(2,1)} custom-call(f32[8,128,128]{2,1,0:T(8,128)S(1)} %get-tuple-element.11.part_ref, bf16[272,128]{1,0:T(8,128)(2,1)S(1)} %collective-permute-done.5.far_ref, bf16[272,128]{1,0:T(8,128)(2,1)S(1)} %collective-permute-done.6.near_ref), custom_call_target="tpu_custom_call" | custom-call | tf_op jit(solution)/shard_map/pallas_call | solution.py:352
  (1 shorter events, 0.0 us)
Async XLA Ops:
  0.6 21.8 %collective-permute-start = (f32[128,256]{1,0:T(8,128)}, f32[128,256]{1,0:T(8,128)S(1)}, u32[]{:S(2)}, u32[]{:S(2)}) collective-permute-start(f32[128,256]{1,0:T(8,128)} %z_ref), channel_id=1, source_target_pairs={{8,0},{16,8},{24,16},{32,24},{40,32},{48,40},{56,48},{64,56},{72,6... | collective-permute-start | bytes 393224 | tf_op jit(solution)/shard_map/ppermute | solution.py:312
  3.9 18.6 %copy-start.1 = (f32[128,256]{1,0:T(8,128)S(1)}, f32[128,256]{1,0:T(8,128)}, u32[]{:S(2)}) copy-start(f32[128,256]{1,0:T(8,128)} %z_ref) | copy-start | bytes 393220
  3.9 41.0 %all-to-all-start = ((bf16[576,2,128]{2,1,0:T(2,128)(2,1)}), bf16[576,2,128]{2,1,0:T(2,128)(2,1)S(1)}, u32[]{:S(2)}, u32[]{:S(2)}) async-start(bf16[576,2,128]{2,1,0:T(2,128)(2,1)} %bitcast.17), calls=%async_computation | async-start | bytes 589824 | tf_op jit(solution)/shard_map/all_to_all | solution.py:315
  22.6 9.8 %collective-permute-start.3 = (bf16[144,256]{1,0:T(8,128)(2,1)S(1)}, bf16[144,256]{1,0:T(8,128)(2,1)S(1)}, u32[]{:S(2)}, u32[]{:S(2)}) collective-permute-start(bf16[144,256]{1,0:T(8,128)(2,1)S(1)} %shard_map.88), channel_id=1, source_target_pairs={{0,6},{1,7},{2,4},{3,5},{4,2},{5,3},{6,0},{7,1},{8,14},{9,15},{10,... | collective-permute-start | bytes 221192 | tf_op jit(solution)/shard_map/ppermute | solution.py:290
  26.8 7.8 %collective-permute-start.2 = (bf16[144,256]{1,0:T(8,128)(2,1)S(1)}, bf16[144,256]{1,0:T(8,128)(2,1)S(1)}, u32[]{:S(2)}, u32[]{:S(2)}) collective-permute-start(bf16[144,256]{1,0:T(8,128)(2,1)S(1)} %shard_map.88), channel_id=1, source_target_pairs={{0,4},{1,5},{2,6},{3,7},{4,0},{5,1},{6,2},{7,3},{8,12},{9,13},{10,... | collective-permute-start | bytes 221192 | tf_op jit(solution)/shard_map/ppermute | solution.py:290
  29.4 6.5 %collective-permute-start.1 = (bf16[144,256]{1,0:T(8,128)(2,1)S(1)}, bf16[144,256]{1,0:T(8,128)(2,1)S(1)}, u32[]{:S(2)}, u32[]{:S(2)}) collective-permute-start(bf16[144,256]{1,0:T(8,128)(2,1)S(1)} %shard_map.88), channel_id=1, source_target_pairs={{0,2},{1,3},{2,0},{3,1},{4,6},{5,7},{6,4},{7,5},{8,10},{9,11},{10,... | collective-permute-start | bytes 221192 | tf_op jit(solution)/shard_map/ppermute | solution.py:290
  35.9 9.9 %collective-permute-start.4 = (bf16[4,144,256]{2,1,0:T(8,128)(2,1)S(1)}, bf16[4,144,256]{2,1,0:T(8,128)(2,1)S(1)}, u32[]{:S(2)}, u32[]{:S(2)}) collective-permute-start(bf16[4,144,256]{2,1,0:T(8,128)(2,1)S(1)} %pad_maximum_fusion.mine_ref), channel_id=1, source_target_pairs={{0,1},{1,0},{2,3},{3,2},{4,5},{5,4},{6,7},{7,6},{8,9},{9,8},{10,11... | collective-permute-start | bytes 884744 | tf_op jit(solution)/shard_map/ppermute | solution.py:290
  44.8 0.9 %copy-start = (s32[4,3]{1,0:T(4,128)S(1)}, s32[4,3]{1,0:T(4,128)}, u32[]{:S(2)}) copy-start(s32[4,3]{1,0:T(4,128)} %list_ref.1) | copy-start | bytes 148
  47.0 8.7 %collective-permute-start.5 = (bf16[272,128]{1,0:T(8,128)(2,1)S(1)}, bf16[272,128]{1,0:T(8,128)(2,1)S(1)}, u32[]{:S(2)}, u32[]{:S(2)}) collective-permute-start(bf16[272,128]{1,0:T(8,128)(2,1)S(1)} %get-tuple-element.12), channel_id=1, source_target_pairs={{8,16},{24,32},{40,48},{56,64},{72,80},{88,96},{104,112},{120,128}... | collective-permute-start | bytes 208904 | tf_op jit(solution)/shard_map/ppermute | solution.py:286
  52.9 6.2 %collective-permute-start.6 = (bf16[272,128]{1,0:T(8,128)(2,1)S(1)}, bf16[272,128]{1,0:T(8,128)(2,1)S(1)}, u32[]{:S(2)}, u32[]{:S(2)}) collective-permute-start(bf16[272,128]{1,0:T(8,128)(2,1)S(1)} %get-tuple-element.13), channel_id=1, source_target_pairs={{0,8},{16,24},{32,40},{48,56},{64,72},{80,88},{96,104},{112,120},{... | collective-permute-start | bytes 208904 | tf_op jit(solution)/shard_map/ppermute | solution.py:286

commit v6 on v5

--- a/solution.py
+++ b/solution.py
@@ -117,7 +117,7 @@
     out_ref[:ROWS, :] = shade_of(z, pltpu.roll(z, 1, 0), pltpu.roll(z, ROWS - 1, 0)).astype(BF16)
     row = iota((8, TILE), 0)
     border = jnp.where(row < 2, z[:8], jnp.where(row < 4, pltpu.roll(z[ROWS - 8 :], 4, 0), F32(0)))
-    edge = jnp.where(lax.axis_index("bands") == 0, beside_ref[:1], beside_ref[ROWS - 1 :])
+    edge = jnp.where(lax.axis_index("bands") == 0, beside_ref[ROWS - 1 :], beside_ref[:1])
     border = jnp.where(row == 4, edge, border)
     high = border.astype(BF16).astype(F32)
     out_ref[ROWS:, :] = jnp.concatenate([high, border - high], axis=0).astype(BF16)
@@ -193,8 +193,8 @@
                 border_ref[f, 2 * tile + i : 2 * tile + i + 1, :] = exact[f : f + 1]
     first, second, before_last, last, edge = [border_ref[f] for f in range(5)]
     row = iota((8, TILE), 0)
-    first_shade = shade_of(first, jnp.where(row == 0, edge[7:8], pltpu.roll(last, 1, 0)), second)
-    last_shade = shade_of(last, before_last, jnp.where(row == 7, edge[0:1], pltpu.roll(first, 7, 0)))
+    first_shade = shade_of(first, jnp.where(row == 0, edge[0:1], pltpu.roll(last, 1, 0)), second)
+    last_shade = shade_of(last, before_last, jnp.where(row == 7, edge[7:8], pltpu.roll(first, 7, 0)))
 
     cols_of = ones_where((iota((TILE, HALF), 0) >> 1) == iota((TILE, HALF), 1)).astype(BF16)
     for tile in range(TILES):
@@ -306,9 +306,9 @@
         along_taps.transpose(1, 2, 0),
         across_taps[0].T,
     )
-    both, last = ("tile", "bands"), lax.axis_size("bands") - 1
-    owners = [last * t + t for t in range(lax.axis_size("tile"))]
-    pairs = list(zip(owners[1:], owners[:-1])) + [(i + last, j + last) for i, j in zip(owners[:-1], owners[1:])]
+    both, bands = ("tile", "bands"), lax.axis_size("bands")
+    pairs = [(bands * t - 1, bands * t) for t in range(1, lax.axis_size("tile"))]
+    pairs = pairs + [(j, i) for i, j in pairs]
     beside = lax.ppermute(elevation, both, pairs)
     outgoing, elevation = lax.optimization_barrier((outgoing, elevation))
     units = outgoing.reshape(OWNERS * CHUNK // 2, 2, HALF)

time: 60.3 us -> 60.4 us (level)
  waiting for transfers between devices: 13.8 us -> 12.8 us
  starting transfers between devices: 38.8 us -> 39.6 us
    all_to_all x1, waiting for transfers between devices: 7.01 us -> 4.92 us  [shards(): lax.all_to_all(units, 'tile', split_axis=0, concat_axis=0, tiled=True)]
    ppermute x4, starting transfers between devices: 11.7 us -> 12.4 us  [exchange(): lax.ppermute(value, 'bands', [(i, i ^ mask) for i in range(lax.axis_size(...]
    ppermute x2, waiting for transfers between devices: 3.46 us -> 4.16 us  [swap(): return lax.ppermute(value, 'tile', pairs + [(j, i) for i, j in pairs])]
  transfers between devices with their start and end apart: 8 -> 8, of which waited for: 4 -> 3; matrix products, arithmetic and copies ran while one was open for 0% -> 0% of each run, Pallas kernels for 7% -> 8%
where the time goes in v6:
time: 60.4 us; the launch traced here: 59.8 us
  starting transfers between devices  39.6 us (66%)
  waiting for transfers between devices  12.8 us (21%)
  Pallas kernels  6.51 us (11%)
  between operations  0.79 us (1%)
    all_to_all x1, starting transfers between devices, shards(): lax.all_to_all(units, 'tile', split_axis=0, concat_axis=0, tiled=True)  18.5 us
    ppermute x4, starting transfers between devices, exchange(): lax.ppermute(value, 'bands', [(i, i ^ mask) for i in range(lax.axis_size(...  12.4 us
    ppermute x2, starting transfers between devices, swap(): return lax.ppermute(value, 'tile', pairs + [(j, i) for i, j in pairs])  7.98 us
    all_to_all x1, waiting for transfers between devices, shards(): lax.all_to_all(units, 'tile', split_axis=0, concat_axis=0, tiled=True)  4.92 us
    ppermute x2, waiting for transfers between devices, swap(): return lax.ppermute(value, 'tile', pairs + [(j, i) for i, j in pairs])  4.16 us
    ppermute x4, waiting for transfers between devices, exchange(): lax.ppermute(value, 'bands', [(i, i ^ mask) for i in range(lax.axis_size(...  3.76 us
    pallas_call x1, Pallas kernels, shards(): call(prep_kernel, shape((OWNERS * CHUNK, HALF), BF16), [VMEM] * 5, [pltpu...  2.55 us
  transfers between devices with their start and end apart: 8, of which 3 were waited for; matrix products, arithmetic and copies ran while one was open for 0% of the time, Pallas kernels for 8%

profile of v6, /device:TPU:38, one launch (start us, length us, event | category | flops | bytes accessed | tf_op | source)
XLA Modules:
  0.0 59.8 jit_solution(2970481293824292865)
XLA Ops:
  0.6 0.7 %collective-permute-start = (f32[128,256]{1,0:T(8,128)}, f32[128,256]{1,0:T(8,128)S(1)}, u32[]{:S(2)}, u32[]{:S(2)}) collective-permute-start(f32[128,256]{1,0:T(8,128)} %z_ref), channel_id=1, source_target_pairs={{7,8},{15,16},{23,24},{31,32},{39,40},{47,48},{55,56},{63,64},{71,... | collective-permute-start | bytes 393224 | tf_op jit(solution)/shard_map/ppermute | solution.py:312
  1.3 2.6 %shard_map.86 = bf16[1152,128]{1,0:T(8,128)(2,1)} custom-call(bf16[128,768]{1,0:T(8,128)(2,1)} %bitcast.20, s32[2,128]{1,0:T(2,128)} %bitcast.26, s32[2,128]{1,0:T(2,128)} %bitcast.27, bf16[2,4,128]{2,1,0:T(4,128)(2,1)} %bitcast.25, bf16[8,256]{1,0:T(8,128)(2,1)} %bitcast.24), custom_call_target="tpu_custom_call" | custom-call | tf_op jit(solution)/shard_map/pallas_call | solution.py:295
  3.9 0.0 copy-start.1
  3.9 18.5 %all-to-all-start = ((bf16[576,2,128]{2,1,0:T(2,128)(2,1)}), bf16[576,2,128]{2,1,0:T(2,128)(2,1)S(1)}, u32[]{:S(2)}, u32[]{:S(2)}) async-start(bf16[576,2,128]{2,1,0:T(2,128)(2,1)} %bitcast.17), calls=%async_computation | async-start | bytes 589824 | tf_op jit(solution)/shard_map/all_to_all | solution.py:315
  22.4 0.0 collective-permute-done.beside_ref
  22.4 0.0 copy-done.1
  22.4 0.2 shard_map.88
  22.6 5.8 %collective-permute-start.3 = (bf16[144,256]{1,0:T(8,128)(2,1)S(1)}, bf16[144,256]{1,0:T(8,128)(2,1)S(1)}, u32[]{:S(2)}, u32[]{:S(2)}) collective-permute-start(bf16[144,256]{1,0:T(8,128)(2,1)S(1)} %shard_map.88), channel_id=1, source_target_pairs={{0,6},{1,7},{2,4},{3,5},{4,2},{5,3},{6,0},{7,1},{8,14},{9,15},{10,... | collective-permute-start | bytes 221192 | tf_op jit(solution)/shard_map/ppermute | solution.py:290
  28.5 1.9 %collective-permute-start.2 = (bf16[144,256]{1,0:T(8,128)(2,1)S(1)}, bf16[144,256]{1,0:T(8,128)(2,1)S(1)}, u32[]{:S(2)}, u32[]{:S(2)}) collective-permute-start(bf16[144,256]{1,0:T(8,128)(2,1)S(1)} %shard_map.88), channel_id=1, source_target_pairs={{0,4},{1,5},{2,6},{3,7},{4,0},{5,1},{6,2},{7,3},{8,12},{9,13},{10,... | collective-permute-start | bytes 221192 | tf_op jit(solution)/shard_map/ppermute | solution.py:290
  30.4 2.8 %collective-permute-start.1 = (bf16[144,256]{1,0:T(8,128)(2,1)S(1)}, bf16[144,256]{1,0:T(8,128)(2,1)S(1)}, u32[]{:S(2)}, u32[]{:S(2)}) collective-permute-start(bf16[144,256]{1,0:T(8,128)(2,1)S(1)} %shard_map.88), channel_id=1, source_target_pairs={{0,2},{1,3},{2,0},{3,1},{4,6},{5,7},{6,4},{7,5},{8,10},{9,11},{10,... | collective-permute-start | bytes 221192 | tf_op jit(solution)/shard_map/ppermute | solution.py:290
  33.2 0.0 collective-permute-done.3
  33.2 3.8 %collective-permute-done.2 = bf16[144,256]{1,0:T(8,128)(2,1)S(1)} collective-permute-done((bf16[144,256]{1,0:T(8,128)(2,1)S(1)}, bf16[144,256]{1,0:T(8,128)(2,1)S(1)}, u32[]{:S(2)}, u32[]{:S(2)}) %collective-permute-start.2) | collective-permute-done | bytes 73760 | tf_op jit(solution)/shard_map/ppermute | solution.py:290
  37.0 0.0 collective-permute-done.1
  37.0 1.9 %collective-permute-start.4 = (bf16[4,144,256]{2,1,0:T(8,128)(2,1)S(1)}, bf16[4,144,256]{2,1,0:T(8,128)(2,1)S(1)}, u32[]{:S(2)}, u32[]{:S(2)}) collective-permute-start(bf16[4,144,256]{2,1,0:T(8,128)(2,1)S(1)} %pad_maximum_fusion.mine_ref), channel_id=1, source_target_pairs={{0,1},{1,0},{2,3},{3,2},{4,5},{5,4},{6,7},{7,6},{8,9},{9,8},{10,11... | collective-permute-start | bytes 884744 | tf_op jit(solution)/shard_map/ppermute | solution.py:290
  38.9 4.9 %all-to-all-done = bf16[576,2,128]{2,1,0:T(2,128)(2,1)S(1)} async-done(((bf16[576,2,128]{2,1,0:T(2,128)(2,1)}), bf16[576,2,128]{2,1,0:T(2,128)(2,1)S(1)}, u32[]{:S(2)}, u32[]{:S(2)}) %all-to-all-start) | async-done | bytes 294944 | tf_op jit(solution)/shard_map/all_to_all | solution.py:315
  43.8 0.0 copy-start
  43.9 0.9 %shard_map.87.resampled_ref = f32[1024,256]{1,0:T(8,128)S(1)} custom-call(bf16[1152,128]{1,0:T(8,128)(2,1)S(1)} %bitcast.15), custom_call_target="tpu_custom_call" | custom-call | flops 400000000 | bytes 1500000 | tf_op jit(solution)/shard_map/pallas_call | solution.py:321
  44.8 0.0 collective-permute-done.4.theirs_ref
  44.8 0.0 copy-done
  44.8 1.2 %shard_map.89 = (bf16[1024,256]{1,0:T(8,128)(2,1)S(1)}, f32[8,128,128]{2,1,0:T(8,128)S(1)}, bf16[272,128]{1,0:T(8,128)(2,1)S(1)}, bf16[272,128]{1,0:T(8,128)(2,1)S(1)}) custom-call(f32[1024,256]{1,0:T(8,128)S(1)} %shard_map.87.resampled_ref, bf16[4,144,256]{2,1,0:T(8,128)(2,1)S(1)} %pad_maximum_fusion.mine_ref, ...), custom_call_target="tpu_custom_call" | custom-call | tf_op jit(solution)/shard_map/pallas_call | solution.py:328
  46.0 6.1 %collective-permute-start.5 = (bf16[272,128]{1,0:T(8,128)(2,1)S(1)}, bf16[272,128]{1,0:T(8,128)(2,1)S(1)}, u32[]{:S(2)}, u32[]{:S(2)}) collective-permute-start(bf16[272,128]{1,0:T(8,128)(2,1)S(1)} %get-tuple-element.12), channel_id=1, source_target_pairs={{8,16},{24,32},{40,48},{56,64},{72,80},{88,96},{104,112},{120,128}... | collective-permute-start | bytes 208904 | tf_op jit(solution)/shard_map/ppermute | solution.py:286
  52.0 1.9 %collective-permute-start.6 = (bf16[272,128]{1,0:T(8,128)(2,1)S(1)}, bf16[272,128]{1,0:T(8,128)(2,1)S(1)}, u32[]{:S(2)}, u32[]{:S(2)}) collective-permute-start(bf16[272,128]{1,0:T(8,128)(2,1)S(1)} %get-tuple-element.13), channel_id=1, source_target_pairs={{0,8},{16,24},{32,40},{48,56},{64,72},{80,88},{96,104},{112,120},{... | collective-permute-start | bytes 208904 | tf_op jit(solution)/shard_map/ppermute | solution.py:286
  54.0 0.8 %shard_map.90 = bf16[1024,256]{1,0:T(8,128)(2,1)} custom-call(bf16[1024,256]{1,0:T(8,128)(2,1)S(1)} %get-tuple-element.10.finished_ref), custom_call_target="tpu_custom_call" | custom-call | bytes 1000000 | tf_op jit(solution)/shard_map/pallas_call | solution.py:344
  54.8 0.0 collective-permute-done.5.far_ref
  54.8 4.2 %collective-permute-done.6.near_ref = bf16[272,128]{1,0:T(8,128)(2,1)S(1)} collective-permute-done((bf16[272,128]{1,0:T(8,128)(2,1)S(1)}, bf16[272,128]{1,0:T(8,128)(2,1)S(1)}, u32[]{:S(2)}, u32[]{:S(2)}) %collective-permute-start.6) | collective-permute-done | bytes 69664 | tf_op jit(solution)/shard_map/ppermute | solution.py:286
  58.9 0.9 %shard_map.91 = bf16[2,256,256]{2,1,0:T(8,128)(2,1)} custom-call(f32[8,128,128]{2,1,0:T(8,128)S(1)} %get-tuple-element.11.part_ref, bf16[272,128]{1,0:T(8,128)(2,1)S(1)} %collective-permute-done.5.far_ref, bf16[272,128]{1,0:T(8,128)(2,1)S(1)} %collective-permute-done.6.near_ref), custom_call_target="tpu_custom_call" | custom-call | tf_op jit(solution)/shard_map/pallas_call | solution.py:352
  (1 shorter events, 0.0 us)
Async XLA Ops:
  0.6 21.8 %collective-permute-start = (f32[128,256]{1,0:T(8,128)}, f32[128,256]{1,0:T(8,128)S(1)}, u32[]{:S(2)}, u32[]{:S(2)}) collective-permute-start(f32[128,256]{1,0:T(8,128)} %z_ref), channel_id=1, source_target_pairs={{7,8},{15,16},{23,24},{31,32},{39,40},{47,48},{55,56},{63,64},{71,... | collective-permute-start | bytes 393224 | tf_op jit(solution)/shard_map/ppermute | solution.py:312
  3.9 18.6 %copy-start.1 = (f32[128,256]{1,0:T(8,128)S(1)}, f32[128,256]{1,0:T(8,128)}, u32[]{:S(2)}) copy-start(f32[128,256]{1,0:T(8,128)} %z_ref) | copy-start | bytes 393220
  3.9 40.0 %all-to-all-start = ((bf16[576,2,128]{2,1,0:T(2,128)(2,1)}), bf16[576,2,128]{2,1,0:T(2,128)(2,1)S(1)}, u32[]{:S(2)}, u32[]{:S(2)}) async-start(bf16[576,2,128]{2,1,0:T(2,128)(2,1)} %bitcast.17), calls=%async_computation | async-start | bytes 589824 | tf_op jit(solution)/shard_map/all_to_all | solution.py:315
  22.6 10.5 %collective-permute-start.3 = (bf16[144,256]{1,0:T(8,128)(2,1)S(1)}, bf16[144,256]{1,0:T(8,128)(2,1)S(1)}, u32[]{:S(2)}, u32[]{:S(2)}) collective-permute-start(bf16[144,256]{1,0:T(8,128)(2,1)S(1)} %shard_map.88), channel_id=1, source_target_pairs={{0,6},{1,7},{2,4},{3,5},{4,2},{5,3},{6,0},{7,1},{8,14},{9,15},{10,... | collective-permute-start | bytes 221192 | tf_op jit(solution)/shard_map/ppermute | solution.py:290
  28.5 8.5 %collective-permute-start.2 = (bf16[144,256]{1,0:T(8,128)(2,1)S(1)}, bf16[144,256]{1,0:T(8,128)(2,1)S(1)}, u32[]{:S(2)}, u32[]{:S(2)}) collective-permute-start(bf16[144,256]{1,0:T(8,128)(2,1)S(1)} %shard_map.88), channel_id=1, source_target_pairs={{0,4},{1,5},{2,6},{3,7},{4,0},{5,1},{6,2},{7,3},{8,12},{9,13},{10,... | collective-permute-start | bytes 221192 | tf_op jit(solution)/shard_map/ppermute | solution.py:290
  30.4 6.5 %collective-permute-start.1 = (bf16[144,256]{1,0:T(8,128)(2,1)S(1)}, bf16[144,256]{1,0:T(8,128)(2,1)S(1)}, u32[]{:S(2)}, u32[]{:S(2)}) collective-permute-start(bf16[144,256]{1,0:T(8,128)(2,1)S(1)} %shard_map.88), channel_id=1, source_target_pairs={{0,2},{1,3},{2,0},{3,1},{4,6},{5,7},{6,4},{7,5},{8,10},{9,11},{10,... | collective-permute-start | bytes 221192 | tf_op jit(solution)/shard_map/ppermute | solution.py:290
  37.0 7.8 %collective-permute-start.4 = (bf16[4,144,256]{2,1,0:T(8,128)(2,1)S(1)}, bf16[4,144,256]{2,1,0:T(8,128)(2,1)S(1)}, u32[]{:S(2)}, u32[]{:S(2)}) collective-permute-start(bf16[4,144,256]{2,1,0:T(8,128)(2,1)S(1)} %pad_maximum_fusion.mine_ref), channel_id=1, source_target_pairs={{0,1},{1,0},{2,3},{3,2},{4,5},{5,4},{6,7},{7,6},{8,9},{9,8},{10,11... | collective-permute-start | bytes 884744 | tf_op jit(solution)/shard_map/ppermute | solution.py:290
  43.8 0.9 %copy-start = (s32[4,3]{1,0:T(4,128)S(1)}, s32[4,3]{1,0:T(4,128)}, u32[]{:S(2)}) copy-start(s32[4,3]{1,0:T(4,128)} %list_ref.1) | copy-start | bytes 148
  46.0 8.8 %collective-permute-start.5 = (bf16[272,128]{1,0:T(8,128)(2,1)S(1)}, bf16[272,128]{1,0:T(8,128)(2,1)S(1)}, u32[]{:S(2)}, u32[]{:S(2)}) collective-permute-start(bf16[272,128]{1,0:T(8,128)(2,1)S(1)} %get-tuple-element.12), channel_id=1, source_target_pairs={{8,16},{24,32},{40,48},{56,64},{72,80},{88,96},{104,112},{120,128}... | collective-permute-start | bytes 208904 | tf_op jit(solution)/shard_map/ppermute | solution.py:286
  52.0 6.9 %collective-permute-start.6 = (bf16[272,128]{1,0:T(8,128)(2,1)S(1)}, bf16[272,128]{1,0:T(8,128)(2,1)S(1)}, u32[]{:S(2)}, u32[]{:S(2)}) collective-permute-start(bf16[272,128]{1,0:T(8,128)(2,1)S(1)} %get-tuple-element.13), channel_id=1, source_target_pairs={{0,8},{16,24},{32,40},{48,56},{64,72},{80,88},{96,104},{112,120},{... | collective-permute-start | bytes 208904 | tf_op jit(solution)/shard_map/ppermute | solution.py:286
